TPU v7x, 256 devices: a whole 4x4x8 slice. The times are simulated.
256 devices in a mesh: list: 64 (over x, z, core), row: 4 (over y).
Axes of the slice: x: 4, y: 4, z: 8, core: 2. Of those that a mesh axis runs over, the one named last changes fastest.
Arguments:
- queries: bfloat16 [16384, 256], P('list'), may hold values from -6 to 6
- query_owner: int32 [16384], P('list'), may hold values from 0 to 7
- probes: int32 [16384, 4], P('list'), may hold values from 0 to 127, all different within a row; in each aligned block of 256 rows (0 to 255, 256 to 511, ...) at most 16 rows name the same one
- list_slab: bfloat16 [128, 16384, 256], P('list', 'row'), may hold values from -48 to 48
- row_owner: int32 [128, 16384], P('list', 'row'), may hold values from 0 to 7
- proj_in: bfloat16 [512, 1024], P(None, 'row'), may hold values from -0.25 to 0.25
- bias_in: bfloat16 [1024], P('row'), may hold values from -4 to 4
- proj_out: bfloat16 [1024, 256], P('row'), may hold values from -0.1875 to 0.1875
Outputs:
- merged_out: bfloat16 [16384, 256], P('list', 'row')
Inputs may be any that keep to these rules, and one draw needn't show every extreme that they name: Within the rows of one device's block of 256 queries, at most 16 probes name the same list, and that many in some blocks; the 4 probes of a query are distinct.
All inputs are finite; a program needn't handle non-finite values.
Results may differ from a plain program's by a relative error of at most 0.0055.
Values may be sent and summed in bfloat16 or wider, within the bound.
A program may use at most 128 MiB of HBM per device.

v0:
```python
import math

import jax
import jax.numpy as jnp
from jax import lax
from jax.sharding import PartitionSpec as P

SCORE_PEN = 10000.0


def slot_ranking(probe_rows, list_total):
    flat_ids = probe_rows.reshape(-1)
    list_ids = jnp.arange(list_total, dtype=jnp.int32)
    onehot = (flat_ids[:, None] == list_ids[None, :]).astype(jnp.int32)
    before = jnp.cumsum(onehot, axis=0) - onehot
    return (flat_ids, jnp.sum(before * onehot, axis=1))


def body(queries, query_owner, probes, list_slab, row_owner, proj_in, bias_in, proj_out):
    n_list = lax.axis_size("list")
    lists_here = list_slab.shape[0]
    query_count = queries.shape[0]
    feat_width = queries.shape[1]
    probe_count = probes.shape[1]
    list_total = n_list * lists_here
    capacity = 8 * query_count // list_total
    flat_ids, slot_rank = slot_ranking(probes, list_total)
    slot_index = flat_ids * capacity + slot_rank
    request_count = flat_ids.shape[0]
    score_scale = 1.0 / math.sqrt(feat_width)
    slot_table = jnp.full((list_total * capacity,), request_count, dtype=jnp.int32)
    slot_table = slot_table.at[slot_index].set(jnp.arange(request_count, dtype=jnp.int32))
    source = jnp.where(slot_table < request_count, slot_table // probe_count, query_count)
    padded_q = jnp.concatenate([queries, jnp.zeros((1, feat_width), queries.dtype)], axis=0)
    padded_owner = jnp.concatenate([query_owner, jnp.full((1,), -1, dtype=jnp.int32)])
    send_q = padded_q[source].reshape(n_list, lists_here, capacity, feat_width)
    send_owner = padded_owner[source].reshape(n_list, lists_here, capacity)
    recv_q = lax.all_to_all(send_q, "list", split_axis=0, concat_axis=0, tiled=True)
    recv_owner = lax.all_to_all(send_owner, "list", split_axis=0, concat_axis=0, tiled=True)
    item_count = recv_q.shape[2]
    score_grids = []
    maxima = []
    for list_pos in range(lists_here):
        rows_q = recv_q[:, list_pos].reshape(n_list * item_count, feat_width)
        owners = recv_owner[:, list_pos].reshape(n_list * item_count)
        score_grid = (
            jnp.einsum("qe,re->qr", rows_q, list_slab[list_pos], preferred_element_type=jnp.float32)
            * score_scale
        )
        same = (owners[:, None] == row_owner[list_pos][None, :]).astype(jnp.float32)
        score_grid = score_grid - SCORE_PEN * same
        score_grids.append(score_grid)
        maxima.append(jnp.max(score_grid, axis=1).reshape(n_list, item_count))
    row_peak = lax.pmax(jnp.stack(maxima, axis=1), "row")
    sum_terms = []
    ctx_terms = []
    for list_pos in range(lists_here):
        exp_terms = jnp.exp(score_grids[list_pos] - row_peak[:, list_pos].reshape(-1)[:, None])
        sum_terms.append(jnp.sum(exp_terms, axis=1).reshape(n_list, item_count))
        weighted_part = jnp.dot(
            exp_terms.astype(jnp.bfloat16), list_slab[list_pos], preferred_element_type=jnp.float32
        )
        ctx_terms.append(weighted_part.reshape(n_list, item_count, feat_width))
    weight_total = jnp.stack(sum_terms, axis=1)
    weighted = jnp.stack(ctx_terms, axis=1)
    weighted, weight_total = lax.psum((weighted, weight_total), "row")
    context = (weighted / weight_total[..., None]).astype(jnp.bfloat16)
    returned = lax.all_to_all(context, "list", split_axis=0, concat_axis=0, tiled=True)
    flat_back = returned.reshape(list_total * capacity, returned.shape[3])
    picked = (
        flat_back[slot_index]
        .astype(jnp.float32)
        .reshape(query_count, probe_count, returned.shape[3])
    )
    retrieved = jnp.mean(picked, axis=1)
    normed = retrieved * lax.rsqrt(jnp.mean(retrieved * retrieved, axis=1, keepdims=True) + 1e-06)
    joined = jnp.concatenate([queries.astype(jnp.float32), normed], axis=1).astype(jnp.bfloat16)
    hidden = jnp.dot(joined, proj_in, preferred_element_type=jnp.float32) + bias_in.astype(
        jnp.float32
    )
    hidden = jax.nn.gelu(hidden, approximate=True).astype(jnp.bfloat16)
    partial_out = jnp.dot(hidden, proj_out, preferred_element_type=jnp.float32)
    return lax.psum_scatter(partial_out, "row", scatter_dimension=1, tiled=True).astype(
        jnp.bfloat16
    )


def solution(mesh):
    in_specs = (
        P("list", None),
        P("list"),
        P("list", None),
        P("list", "row", None),
        P("list", "row"),
        P(None, "row"),
        P("row"),
        P("row", None),
    )
    out_specs = P("list", "row")
    return jax.shard_map(body, mesh=mesh, in_specs=in_specs, out_specs=out_specs, check_vma=False)
```

profile of v0, /device:TPU:32, one launch (start us, length us, event | category | flops | bytes accessed | tf_op | source)
XLA Modules:
  0.0 281.0 jit_solution(5055727314794269636)
XLA Ops:
  6.5 0.9 copy.16
  7.7 0.7 broadcast_multiply_fusion
  9.1 0.4 fusion.25
  9.5 4.3 %scatter_custom_fusion = s32[2048]{0:T(1024)S(1)} fusion(s32[1024]{0:T(1024)S(1)} %bitcast.66, s32[1024]{0:T(1024)S(1)} %iota.11, s32[]{:T(128)} %constant.24.clone.1), kind=kCustom, calls=%fused_computation.76 | custom fusion | bytes 8196 | tf_op jit(solution)/shard_map/scatter | solution.py:32
  13.9 0.7 pad_add_fusion
  14.6 13.2 %gather_fusion.1 = s32[2048]{0:T(1024)S(1)} fusion(s32[257]{0:T(512)S(1)} %pad_add_fusion, s32[2048]{0:T(1024)S(1)} %fusion.51), kind=kCustom, calls=%fused_computation.1 | custom fusion | bytes 24576 | tf_op jit(solution)/shard_map/gather | solution.py:37
  27.7 0.8 reshape.87
  28.5 11.6 %all-to-all-start.1 = ((s32[64,2,16]{2,1,0:T(2,128)}), s32[64,2,16]{2,1,0:T(2,128)S(1)}, u32[]{:S(2)}, u32[]{:S(2)}) async-start(s32[64,2,16]{2,1,0:T(2,128)} %reshape.87), calls=%async_computation.1 | async-start | bytes 131072 | tf_op jit(solution)/shard_map/all_to_all | solution.py:39
  40.1 0.9 concatenate.10
  41.0 9.0 %gather_fusion = bf16[2048,256]{1,0:T(8,128)(2,1)} fusion(bf16[257,256]{1,0:T(8,128)(2,1)S(1)} %concatenate.10, s32[2048]{0:T(1024)S(1)} %fusion.51), kind=kCustom, calls=%fused_computation | custom fusion | bytes 2105344 | tf_op jit(solution)/shard_map/gather | solution.py:36
  50.0 10.3 %all-to-all-start = ((bf16[64,2,16,256]{3,2,1,0:T(8,128)(2,1)}), bf16[64,2,16,256]{3,2,1,0:T(8,128)(2,1)S(1)}, u32[]{:S(2)}, u32[]{:S(2)}) async-start(bf16[64,2,16,256]{3,2,1,0:T(8,128)(2,1)} %bitcast.5), calls=%async_computation | async-start | bytes 2097152 | tf_op jit(solution)/shard_map/all_to_all | solution.py:38
  60.8 27.4 %all-to-all-done = bf16[64,2,16,256]{3,2,1,0:T(8,128)(2,1)S(1)} async-done(((bf16[64,2,16,256]{3,2,1,0:T(8,128)(2,1)}), bf16[64,2,16,256]{3,2,1,0:T(8,128)(2,1)S(1)}, u32[]{:S(2)}, u32[]{:S(2)}) %all-to-all-start) | async-done | bytes 1048608 | tf_op jit(solution)/shard_map/all_to_all | solution.py:38
  88.3 9.1 %fusion.4 = (f32[1024]{0:T(1024)S(1)}, f32[1024,4096]{1,0:T(8,128)}) fusion(s32[4096]{0:T(1024)S(1)} %bitcast.63, s32[1024]{0:T(1024)S(1)} %eq.67, bf16[1024,256]{1,0:T(8,128)(2,1)S(1)} %bitcast.60, bf16[2,4096,256]{2,1,0:T(8,128)(2,1)} %param.11), kind=kOutput, calls=%fused_computation.12 | convolution fusion | flops 2168454144 | bytes 19423232 | tf_op jit(solution)/shard_map/qe,re->qr/dot_general | solution.py:47
  97.6 9.1 %fusion.5 = (f32[1024]{0:T(1024)S(1)}, f32[1024,4096]{1,0:T(8,128)}) fusion(s32[4096]{0:T(1024)S(1)} %bitcast.61, s32[1024]{0:T(1024)S(1)} %eq.72, bf16[1024,256]{1,0:T(8,128)(2,1)S(1)} %bitcast.59, bf16[2,4096,256]{2,1,0:T(8,128)(2,1)} %param.11), kind=kOutput, calls=%fused_computation.13 | convolution fusion | flops 2168454144 | bytes 19423232 | tf_op jit(solution)/shard_map/qe,re->qr/dot_general | solution.py:47
  106.8 17.2 %pmax.7 = f32[64,2,16]{0,2,1:T(8,128)S(1)} all-reduce(f32[64,2,16]{0,2,1:T(8,128)S(1)} %pad_maximum_fusion.1), channel_id=1, replica_groups=mesh['list'=64,'row'=4] {'row'}, use_global_device_ids=true, to_apply=%region_6.7 | all-reduce | flops 2048 | bytes 16384 | tf_op jit(solution)/shard_map/pmax | solution.py:54
  124.3 9.6 %fusion = (f32[1024]{0:T(1024)S(1)}, bf16[1024,4096]{1,0:T(8,128)(2,1)S(1)}) fusion(f32[1024,4096]{1,0:T(8,128)} %get-tuple-element.20, f32[1024]{0:T(1024)S(1)} %sub.39, s32[4096]{0:T(1024)S(1)} %bitcast.64, s32[1024]{0:T(1024)S(1)} %eq.67), kind=kLoop, calls=%fused_computation.8 | loop fusion | flops 29359104 | bytes 25194496 | tf_op jit(solution)/shard_map/reduce_sum | solution.py:59
  133.9 2.3 fusion.18
  136.3 0.3 slice-done.3
  136.6 5.4 %fusion.2 = (f32[1024]{0:T(1024)S(1)}, bf16[1024,4096]{1,0:T(8,128)(2,1)S(1)}) fusion(f32[1024,4096]{1,0:T(8,128)S(1)} %bitcast.56, f32[1024]{0:T(1024)S(1)} %sub.42, s32[4096]{0:T(1024)S(1)} %bitcast.62, s32[1024]{0:T(1024)S(1)} %eq.72), kind=kLoop, calls=%fused_computation.10 | loop fusion | flops 29359104 | bytes 25194496 | tf_op jit(solution)/shard_map/reduce_sum | solution.py:59
  142.0 2.3 fusion.21
  144.4 1.5 pad_maximum_fusion
  146.2 14.4 %psum.15 = f32[64,2,16]{0,2,1:T(8,128)S(1)} all-reduce(f32[64,2,16]{0,2,1:T(8,128)S(1)} %pad_maximum_fusion.2), channel_id=1, replica_groups=mesh['list'=64,'row'=4] {'row'}, use_global_device_ids=true, to_apply=%region_10.11 | all-reduce | flops 2048 | bytes 16384 | tf_op jit(solution)/shard_map/psum | solution.py:66
  160.6 44.8 %all-reduce.3.cloned.1.call-done = f32[64,2,16,256]{3,2,0,1:T(8,128)} async-done(((f32[64,2,16,256]{3,2,0,1:T(8,128)}), f32[64,2,16,256]{3,2,0,1:T(8,128)}) %all-reduce.3.cloned.1.call-update) | async-done | bytes 2097168 | tf_op jit(solution)/shard_map/psum | solution.py:66
  205.4 1.9 divide_convert_fusion
  207.4 1.1 copy.27
  208.5 10.5 %all-to-all-start.2 = ((bf16[64,2,16,256]{3,2,1,0:T(8,128)(2,1)}), bf16[64,2,16,256]{3,2,1,0:T(8,128)(2,1)S(1)}, u32[]{:S(2)}, u32[]{:S(2)}) async-start(bf16[64,2,16,256]{3,2,1,0:T(8,128)(2,1)} %copy.27), calls=%async_computation.2 | async-start | bytes 2097152 | tf_op jit(solution)/shard_map/all_to_all | solution.py:68
  219.1 27.8 %all-to-all-done.2 = bf16[64,2,16,256]{3,2,1,0:T(8,128)(2,1)S(1)} async-done(((bf16[64,2,16,256]{3,2,1,0:T(8,128)(2,1)}), bf16[64,2,16,256]{3,2,1,0:T(8,128)(2,1)S(1)}, u32[]{:S(2)}, u32[]{:S(2)}) %all-to-all-start.2) | async-done | bytes 1048608 | tf_op jit(solution)/shard_map/all_to_all | solution.py:68
  246.9 3.9 %gather_fusion.2 = bf16[1024,256]{1,0:T(8,128)(2,1)S(1)} fusion(bf16[2048,256]{1,0:T(8,128)(2,1)S(1)} %bitcast.54, s32[1024]{0:T(1024)S(1)} %broadcast_clamp_fusion), kind=kCustom, calls=%fused_computation.2 | custom fusion | bytes 1052672 | tf_op jit(solution)/shard_map/gather | solution.py:71
  251.1 0.6 reduce_sum.51
  252.0 1.2 fusion.36
  253.2 19.5 %reduce-scatter.2.cloned.1.call-done = f32[256,64]{0,1:T(8,128)} async-done(((f32[256,256]{0,1:T(8,128)}), f32[256,64]{0,1:T(8,128)}) %reduce-scatter.2.cloned.1.call-update) | async-done | bytes 65552 | tf_op jit(solution)/shard_map/reduce_scatter | solution.py:83
  272.7 1.5 convert_element_type.45
  (66 shorter events, 3.1 us)
Async XLA Ops:
  6.5 245.4 %copy-start = (bf16[512,256]{1,0:T(8,128)(2,1)S(1)}, bf16[512,256]{1,0:T(8,128)(2,1)}, u32[]{:S(2)}) copy-start(bf16[512,256]{1,0:T(8,128)(2,1)} %param.13) | copy-start | bytes 786436
  6.5 53.9 %copy-start.2 = (s32[2,4096]{1,0:T(2,128)S(1)}, s32[2,4096]{1,0:T(2,128)}, u32[]{:S(2)}) copy-start(s32[2,4096]{1,0:T(2,128)} %param.12) | copy-start | bytes 98308
  28.5 21.5 %all-to-all-start.1 = ((s32[64,2,16]{2,1,0:T(2,128)}), s32[64,2,16]{2,1,0:T(2,128)S(1)}, u32[]{:S(2)}, u32[]{:S(2)}) async-start(s32[64,2,16]{2,1,0:T(2,128)} %reshape.87), calls=%async_computation.1 | async-start | bytes 131072 | tf_op jit(solution)/shard_map/all_to_all | solution.py:39
  50.0 38.2 %all-to-all-start = ((bf16[64,2,16,256]{3,2,1,0:T(8,128)(2,1)}), bf16[64,2,16,256]{3,2,1,0:T(8,128)(2,1)S(1)}, u32[]{:S(2)}, u32[]{:S(2)}) async-start(bf16[64,2,16,256]{3,2,1,0:T(8,128)(2,1)} %bitcast.5), calls=%async_computation | async-start | bytes 2097152 | tf_op jit(solution)/shard_map/all_to_all | solution.py:38
  60.3 145.1 %all-reduce.3.cloned.1.call-start = ((), (), s32[]{:S(2)}) async-start(), calls=%async_computation.4 | async-start | bytes 4194304 | tf_op jit(solution)/shard_map/psum | solution.py:66
  124.3 9.6 %copy-start.3 = (bf16[2,4096,256]{2,1,0:T(8,128)(2,1)S(1)}, bf16[2,4096,256]{2,1,0:T(8,128)(2,1)}, u32[]{:S(2)}) copy-start(bf16[2,4096,256]{2,1,0:T(8,128)(2,1)} %param.11) | copy-start | bytes 12582916
  124.3 12.0 %slice-start = ((s8[16777216]{0:T(1024)(128)(4,1)}), s8[4194304]{0:T(1024)(128)(4,1)S(1)}, s32[]{:S(2)}) async-start(s8[16777216]{0:T(1024)(128)(4,1)} %bitcast.55), calls=%async_computation.6 | async-start | bytes 8388608
  124.3 12.0 %slice-start.1 = ((s8[16777216]{0:T(1024)(128)(4,1)}), s8[4194304]{0:T(1024)(128)(4,1)S(1)}, s32[]{:S(2)}) async-start(s8[16777216]{0:T(1024)(128)(4,1)} %bitcast.55), calls=%async_computation.7 | async-start | bytes 8388608
  124.3 12.0 %slice-start.2 = ((s8[16777216]{0:T(1024)(128)(4,1)}), s8[4194304]{0:T(1024)(128)(4,1)S(1)}, s32[]{:S(2)}) async-start(s8[16777216]{0:T(1024)(128)(4,1)} %bitcast.55), calls=%async_computation.8 | async-start | bytes 8388608
  133.9 2.6 slice-start.3
  142.0 77.0 %copy-start.5 = (bf16[256]{0:T(256)(128)(2,1)S(1)}, bf16[256]{0:T(256)(128)(2,1)}, u32[]{:S(2)}) copy-start(bf16[256]{0:T(256)(128)(2,1)} %param.14) | copy-start | bytes 1540
  142.0 109.9 %copy-start.1 = (bf16[256,256]{1,0:T(8,128)(2,1)S(1)}, bf16[256,256]{1,0:T(8,128)(2,1)}, u32[]{:S(2)}) copy-start(bf16[256,256]{1,0:T(8,128)(2,1)} %param.8) | copy-start | bytes 393220
  142.0 109.9 %copy-start.4 = (bf16[256,256]{1,0:T(8,128)(2,1)S(1)}, bf16[256,256]{1,0:T(8,128)(2,1)}, u32[]{:S(2)}) copy-start(bf16[256,256]{1,0:T(8,128)(2,1)} %param.15) | copy-start | bytes 393220
  208.5 38.3 %all-to-all-start.2 = ((bf16[64,2,16,256]{3,2,1,0:T(8,128)(2,1)}), bf16[64,2,16,256]{3,2,1,0:T(8,128)(2,1)S(1)}, u32[]{:S(2)}, u32[]{:S(2)}) async-start(bf16[64,2,16,256]{3,2,1,0:T(8,128)(2,1)} %copy.27), calls=%async_computation.2 | async-start | bytes 2097152 | tf_op jit(solution)/shard_map/all_to_all | solution.py:68
  219.0 53.7 %reduce-scatter.2.cloned.1.call-start = ((), (), s32[]{:S(2)}) async-start(), calls=%async_computation.5 | async-start | bytes 327680 | tf_op jit(solution)/shard_map/reduce_scatter | solution.py:83
Sparse Core Ops, SparseCore 0:
  146.0 59.4 all-reduce.2
  253.3 19.3 reduce-scatter.1
where the time goes:
time: 282 us; the launch traced here: 281 us
  waiting for transfers between devices  120 us (43%)
  local copies, waits for them, and re-layouts  36.8 us (13%)
  starting transfers between devices  32.4 us (11%)
  blocking collectives  31.6 us (11%)
  matrix products  24.1 us (9%)
  other arithmetic  22.7 us (8%)
  between operations  13.8 us (5%)
    psum x1, waiting for transfers between devices, body(): weighted, weight_total = lax.psum((weighted, weight_total), 'row')  44.8 us
    all_to_all x1, waiting for transfers between devices, body(): lax.all_to_all(context, 'list', split_axis=0, concat_axis=0, tiled=True)  27.8 us
    all_to_all x1, waiting for transfers between devices, body(): lax.all_to_all(send_q, 'list', split_axis=0, concat_axis=0, tiled=True)  27.4 us
    reduce_scatter x1, waiting for transfers between devices, body(): lax.psum_scatter(partial_out, 'row', scatter_dimension=1, tiled=True)  19.5 us
    dot_general x2, matrix products, body(): jnp.einsum('qe,re->qr', rows_q, list_slab[list_pos], preferred_element_ty...  18.2 us
    pmax x1, blocking collectives, body(): row_peak = lax.pmax(jnp.stack(maxima, axis=1), 'row')  17.2 us
    reduce_sum x2, other arithmetic, body(): sum_terms.append(jnp.sum(exp_terms, axis=1).reshape(n_list, item_count))  15 us
    psum x1, blocking collectives, body(): weighted, weight_total = lax.psum((weighted, weight_total), 'row')  14.4 us
  transfers between devices with their start and end apart: 5, of which 4 were waited for; matrix products, arithmetic and copies ran while one was open for 4% of the time, Pallas kernels for 0%

commit v1 on v0

v1 whole, which is shorter than its diff:
```python
import math

import jax
import jax.numpy as jnp
from jax import lax
from jax.experimental import pallas as pl
from jax.experimental.pallas import tpu as pltpu
from jax.sharding import PartitionSpec as P

SCORE_PEN = 10000.0
LOG2E = math.log2(math.e)
NX, NZ, NC, NY = 4, 8, 2, 4
CAP = 16
TILE = 512
MESH = pl.DeviceIdType.MESH
F32 = jnp.float32
BF16 = jnp.bfloat16


def xor(a, b, bits):
    out = 0
    for i in range(bits):
        out = out + ((a // 2**i + b // 2**i) % 2) * 2**i
    return out


def nt_dot(a, b):
    return lax.dot_general(a, b, (((1,), (1,)), ((), ())), preferred_element_type=F32)


def kernel(
    q_ref, owner_ref, probes_ref, slab_hbm, rowner_ref, win_ref, bias_ref, wout_ref,
    out_ref,
    slab, kt, rcol, onehot, onehot_t, send_q, send_o, recv_q, recv_o, own_o, qt, scores, acc,
    part, lse, rpart, rlse, ctx, ret, pq, rpq, blk, rblk, wi, wo, bi,
    slab_sem, a2a_s, a2a_r, o_s, o_r, ag_s, ag_r, ago_s, ago_r, w_s, w_r, rs_s, rs_r, rl_s, rl_r,
    ret_s, ret_r, pq_s, pq_r, blk_s, blk_r, loc_sem,
):
    nk = NZ * NC
    nq = nk * CAP
    rows = slab.shape[1]
    feat = slab.shape[2]
    tile = scores.shape[2]
    ntile = rows // tile
    li = lax.axis_index("list")
    y = lax.axis_index("row")
    core = li % NC
    z = (li // NC) % NZ
    x = li // (NC * NZ)

    def partner(k):
        dz, dc = k // NC, k % NC
        return (xor(x, xor(y, dz % 4, 2), 2) * NZ + xor(z, dz, 3)) * NC + (core + dc) % NC

    def peer(j):
        return (y + j) % NY

    barrier = pltpu.get_barrier_semaphore()
    for j in (1, 2, 3):
        pl.semaphore_signal(barrier, inc=1, device_id=(li, peer(j)), device_id_type=MESH)

    @pl.when(y != 0)
    def _():
        pl.semaphore_signal(barrier, inc=1, device_id=(partner(0), y), device_id_type=MESH)

    def sig(k, c):
        pl.semaphore_signal(barrier, inc=1, device_id=(partner(k), y), device_id_type=MESH)
        return c

    lax.fori_loop(1, nk, sig, 0)

    slab_copies = [pltpu.make_async_copy(slab_hbm.at[l], slab.at[l], slab_sem.at[l]) for l in range(2)]
    for c in slab_copies:
        c.start()

    nl = 2 * nk
    row = lax.broadcasted_iota(jnp.int32, (nl, q_ref.shape[0]), 0)
    kk = row // 2
    dz = kk // NC
    xd = x ^ y ^ (dz & 3)
    zd = z ^ dz
    cd = (core + kk) % NC
    lvec = ((xd * NZ + zd) * NC + cd) * 2 + row % 2
    hit = probes_ref[0:1, :] == lvec
    for j in range(1, 4):
        hit = hit | (probes_ref[j : j + 1, :] == lvec)
    hits = jnp.where(hit, 1.0, 0.0).astype(F32)
    qn = q_ref.shape[0]
    before = jnp.where(
        lax.broadcasted_iota(jnp.int32, (qn, qn), 0) < lax.broadcasted_iota(jnp.int32, (qn, qn), 1), 1.0, 0.0
    ).astype(BF16)
    rank = jnp.dot(hits.astype(BF16), before, preferred_element_type=F32)
    rank = jnp.where(hit, rank, -1.0)
    slot = lax.broadcasted_iota(jnp.int32, (CAP, qn), 0).astype(F32)
    for r in range(nl):
        onehot[r // 2, r % 2] = jnp.where(rank[r : r + 1, :] == slot, 1.0, 0.0).astype(BF16)
    oh = onehot[...].reshape(nl * CAP, qn)
    picked = jnp.dot(oh, q_ref[...], preferred_element_type=F32) * (1.0 / math.sqrt(feat))
    send_q[...] = picked.astype(BF16).reshape(send_q.shape)
    own8 = jnp.broadcast_to((owner_ref[...] + 1).astype(F32), (8, qn)).astype(BF16)
    for i in range(2):
        send_o[i : i + 1, :] = nt_dot(own8, onehot[:, i].reshape(nq, qn))[0:1, :]
    bi[y] = jnp.broadcast_to(bias_ref[...].astype(F32), (8, bias_ref.shape[1]))

    pl.semaphore_wait(barrier, 19 - 16 + nk - (1 - (y + 3) // 4))

    def q_copy(k):
        return pltpu.make_async_remote_copy(
            src_ref=send_q.at[k], dst_ref=recv_q.at[y, k], send_sem=a2a_s.at[k], recv_sem=a2a_r.at[k],
            device_id=(partner(k), y), device_id_type=MESH)

    def o_copy(k):
        return pltpu.make_async_remote_copy(
            src_ref=send_o, dst_ref=recv_o.at[k], send_sem=o_s.at[k], recv_sem=o_r.at[k],
            device_id=(partner(k), y), device_id_type=MESH)

    q_self = pltpu.make_async_copy(send_q.at[0], recv_q.at[y, 0], a2a_r.at[0])
    o_self = pltpu.make_async_copy(send_o, recv_o.at[0], o_r.at[0])

    @pl.when(y == 0)
    def _():
        q_self.start()
        o_self.start()

    @pl.when(y != 0)
    def _():
        q_copy(0).start()
        o_copy(0).start()

    def a2a_start(k, c):
        q_copy(k).start()
        o_copy(k).start()
        return c

    lax.fori_loop(1, nk, a2a_start, 0)

    def w_copies(j):
        dev = (li, peer(j))
        return [
            pltpu.make_async_remote_copy(
                src_ref=s, dst_ref=d.at[y], send_sem=w_s.at[n, j - 1], recv_sem=w_r.at[n, j - 1],
                device_id=dev, device_id_type=MESH)
            for n, (s, d) in enumerate(((win_ref, wi), (wout_ref, wo), (bi.at[y], bi)))
        ]

    weight_copies = [c for j in (1, 2, 3) for c in w_copies(j)]
    for c in weight_copies:
        c.start()
    local = [pltpu.make_async_copy(win_ref, wi.at[y], loc_sem.at[0]), pltpu.make_async_copy(wout_ref, wo.at[y], loc_sem.at[1])]
    for c in local:
        c.start()

    onehot_t[...] = oh.astype(F32).T.astype(BF16)
    for l in range(2):
        slab_copies[l].wait()

        def prep(t, c):
            blkk = slab[l, pl.ds(t * tile, tile), :]
            kt[l, t, 0:feat, :] = blkk.astype(F32).T.astype(BF16)
            kt[l, t, feat : feat + 16, :] = jnp.ones((16, tile), BF16)
            for h in range(tile // 128):
                rr = rowner_ref[l : l + 1, pl.ds(t * tile + h * 128, 128)].astype(F32)
                rcol[l, pl.ds(t * tile + h * 128, 128), :] = jnp.broadcast_to(rr, (128, 128)).T
            return c

        lax.fori_loop(0, ntile, prep, 0)

    @pl.when(y == 0)
    def _():
        q_self.wait()
        o_self.wait()

    @pl.when(y != 0)
    def _():
        q_copy(0).wait()
        o_copy(0).wait()

    def a2a_wait(k, c):
        q_copy(k).wait()
        o_copy(k).wait()
        return c

    lax.fori_loop(1, nk, a2a_wait, 0)
    lane_k = lax.broadcasted_iota(jnp.int32, (2, nq), 1) // CAP
    total_o = jnp.zeros((2, nq), F32)
    for k in range(nk):
        total_o = total_o + jnp.where(lane_k == k, recv_o[k], 0.0)
    own_o[y] = total_o - 1.0

    def ag_copies(j):
        dev = (li, peer(j))
        return [
            pltpu.make_async_remote_copy(
                src_ref=s.at[y], dst_ref=s.at[y], send_sem=ss.at[j - 1], recv_sem=rr.at[j - 1],
                device_id=dev, device_id_type=MESH)
            for s, ss, rr in ((recv_q, ag_s, ag_r), (own_o, ago_s, ago_r))
        ]

    ag = {j: ag_copies(j) for j in (1, 3, 2)}
    for j in (1, 3, 2):
        for c in ag[j]:
            c.start()

    order = [(0, 0), (1, 0), (3, 0), (1, 1), (3, 1), (2, 0), (2, 1), (0, 1)]
    arrived = {0}
    rs_sends = []

    def rs_copies(j, l):
        dev = (li, peer(j))
        return [
            pltpu.make_async_remote_copy(
                src_ref=part.at[peer(j), l], dst_ref=rpart.at[j - 1, l], send_sem=rs_s.at[j - 1, l],
                recv_sem=rs_r.at[j - 1, l], device_id=dev, device_id_type=MESH),
            pltpu.make_async_remote_copy(
                src_ref=lse.at[peer(j), l], dst_ref=rlse.at[j - 1, l], send_sem=rl_s.at[j - 1, l],
                recv_sem=rl_r.at[j - 1, l], device_id=dev, device_id_type=MESH),
        ]

    def score_tile(n, l, t, own_row, m):
        s = jnp.dot(slab[l, pl.ds(t * tile, tile), :], qt[n % 2], preferred_element_type=F32)
        rc = rcol[l, pl.ds(t * tile, tile), :]
        halves = []
        for h in range(nq // 128):
            cols = slice(h * 128, (h + 1) * 128)
            sh = s[:, cols]
            sh = jnp.where(rc == own_row[:, cols], sh - SCORE_PEN, sh)
            scores[n % 2, t, :, cols] = sh
            halves.append(jnp.max(sh.reshape(tile // 8, 8, 128), axis=0))
        return jnp.maximum(m, jnp.concatenate(halves, axis=1))

    def sum_tile(n, l, t, peak):
        w = jnp.exp2(((scores[n % 2, t] - peak) * LOG2E).astype(BF16))
        acc[...] += jnp.dot(kt[l, t], w, preferred_element_type=F32)

    peak = None
    for n in range(len(order) + 1):
        own_row = None
        if n < len(order):
            j, l = order[n]
            src = peer(NY - j)
            if j not in arrived:
                for c in ag[j]:
                    c.wait_recv()
                arrived.add(j)
            src = peer(NY - j)
            qt[n % 2] = recv_q[src, :, l].reshape(nq, feat).astype(F32).T.astype(BF16)
            own_row = own_o[src, l : l + 1, :]
        if n > 0:
            acc[...] = jnp.zeros_like(acc)
        prev_peak = peak

        def stage(t, m, n=n, own_row=own_row, prev_peak=prev_peak):
            if n > 0:
                sum_tile(n - 1, order[n - 1][1], t, prev_peak)
            if n < len(order):
                m = score_tile(n, order[n][1], t, own_row, m)
            return m

        m = lax.fori_loop(0, ntile, stage, jnp.full((8, nq), -jnp.inf, F32))
        if n > 0:
            pj, pl_ = order[n - 1]
            psrc = peer(NY - pj)
            total = acc[feat : feat + 1, :]
            mean = acc[0:feat, :] / total
            part[psrc, pl_] = mean.T.astype(BF16)
            lse[psrc, pl_] = prev_peak + jnp.log(total)
            if pj != 0:
                for c in rs_copies(NY - pj, pl_):
                    c.start()
                    rs_sends.append(c)
        if n < len(order):
            peak = jnp.max(m, axis=0, keepdims=True)

    for l in range(2):
        for j in (1, 3, 2):
            for c in rs_copies(j, l):
                c.wait_recv()
        ls = [lse[y, l]] + [rlse[j - 1, l] for j in (1, 2, 3)]
        top = jnp.maximum(jnp.maximum(ls[0], ls[1]), jnp.maximum(ls[2], ls[3]))
        es = [jnp.exp(v - top) for v in ls]
        inv = 1.0 / (es[0] + es[1] + es[2] + es[3])
        cols = [jnp.broadcast_to(e * inv, (128, nq)).T for e in es]
        srcs = [part[y, l]] + [rpart[j - 1, l] for j in (1, 2, 3)]
        for h in range(feat // 128):
            cs = slice(h * 128, (h + 1) * 128)
            val = cols[0] * srcs[0][:, cs].astype(F32)
            for a in range(1, 4):
                val = val + cols[a] * srcs[a][:, cs].astype(F32)
            ctx[:, l, :, cs] = val.astype(BF16).reshape(nk, CAP, 128)

    def ret_copy(k):
        return pltpu.make_async_remote_copy(
            src_ref=ctx.at[k], dst_ref=ret.at[k], send_sem=ret_s.at[k], recv_sem=ret_r.at[k],
            device_id=(partner(k), y), device_id_type=MESH)

    ret_self = pltpu.make_async_copy(ctx.at[0], ret.at[0], ret_r.at[0])

    @pl.when(y == 0)
    def _():
        ret_self.start()

    @pl.when(y != 0)
    def _():
        ret_copy(0).start()

    def ret_start(k, c):
        ret_copy(k).start()
        return c

    lax.fori_loop(1, nk, ret_start, 0)

    @pl.when(y == 0)
    def _():
        ret_self.wait()

    @pl.when(y != 0)
    def _():
        ret_copy(0).wait()

    def ret_wait(k, c):
        ret_copy(k).wait()
        return c

    lax.fori_loop(1, nk, ret_wait, 0)

    share = jnp.dot(onehot_t[...], ret[...].reshape(nl * CAP, feat), preferred_element_type=F32) * 0.25
    qb = qn // NY
    pq[...] = share.astype(BF16).reshape(NY, qb, feat)
    pq_copies = {}
    for j in (1, 2, 3):
        pq_copies[j] = pltpu.make_async_remote_copy(
            src_ref=pq.at[peer(j)], dst_ref=rpq.at[j - 1], send_sem=pq_s.at[j - 1], recv_sem=pq_r.at[j - 1],
            device_id=(li, peer(j)), device_id_type=MESH)
        pq_copies[j].start()
    for c in weight_copies:
        c.wait()
    for c in local:
        c.wait()
    mine = q_ref[pl.ds(pl.multiple_of(y * qb, qb), qb), :]
    for j in (1, 2, 3):
        pq_copies[j].wait()
    retrieved = pq[y].astype(F32)
    for j in (1, 2, 3):
        retrieved = retrieved + rpq[j - 1].astype(F32)
    normed = retrieved * lax.rsqrt(jnp.mean(retrieved * retrieved, axis=1, keepdims=True) + 1e-06)
    normed = normed.astype(BF16)
    res = jnp.zeros((qb, feat), F32)
    for b in range(NY):
        hid = jnp.dot(mine, wi[b, 0:feat, :], preferred_element_type=F32)
        hid = hid + jnp.dot(normed, wi[b, feat : 2 * feat, :], preferred_element_type=F32)
        hid = jax.nn.gelu(hid + bi[b, 0:1, :], approximate=True).astype(BF16)
        res = res + jnp.dot(hid, wo[b], preferred_element_type=F32)
    ob = feat // NY
    for b in range(NY):
        blk[b, :, 0:ob] = res[:, b * ob : (b + 1) * ob].astype(BF16)
        blk[b, :, ob:128] = jnp.zeros((qb, 128 - ob), BF16)
    blk_copies = {}
    for j in (1, 2, 3):
        blk_copies[j] = pltpu.make_async_remote_copy(
            src_ref=blk.at[peer(j)], dst_ref=rblk.at[y], send_sem=blk_s.at[j - 1], recv_sem=blk_r.at[j - 1],
            device_id=(li, peer(j)), device_id_type=MESH)
        blk_copies[j].start()
    out_ref[pl.ds(pl.multiple_of(y * qb, qb), qb), :] = blk[y][:, 0:ob]
    for j in (1, 2, 3):
        for c in ag[j]:
            c.wait_send()
    for c in rs_sends:
        c.wait_send()
    for j in (1, 2, 3):
        blk_copies[j].wait()
        src = peer(NY - j)
        out_ref[pl.ds(pl.multiple_of(src * qb, qb), qb), :] = rblk[src][:, 0:ob]


def body(queries, query_owner, probes, list_slab, row_owner, proj_in, bias_in, proj_out):
    qn, feat = queries.shape
    lists, rows = list_slab.shape[0], list_slab.shape[1]
    nk = NZ * NC
    nq = nk * CAP
    nl = 2 * nk
    tile = min(TILE, rows)
    nt = rows // tile
    hid = proj_in.shape[1]
    qb = qn // NY
    vm = pltpu.VMEM
    dma = pltpu.SemaphoreType.DMA
    vspec = pl.BlockSpec(memory_space=pltpu.VMEM)
    return pl.pallas_call(
        kernel,
        out_shape=jax.ShapeDtypeStruct((qn, feat // NY), BF16),
        in_specs=[vspec, vspec, vspec, pl.BlockSpec(memory_space=pl.ANY), vspec, vspec, vspec, vspec],
        out_specs=vspec,
        scratch_shapes=[
            vm((lists, rows, feat), BF16),
            vm((lists, nt, feat + 16, tile), BF16),
            vm((lists, rows, 128), F32),
            vm((nk, 2, CAP, qn), BF16),
            vm((qn, nl * CAP), BF16),
            vm((nk, 2, CAP, feat), BF16),
            vm((2, nq), F32),
            vm((NY, nk, 2, CAP, feat), BF16),
            vm((nk, 2, nq), F32),
            vm((NY, 2, nq), F32),
            vm((2, feat, nq), BF16),
            vm((2, nt, tile, nq), F32),
            vm((feat + 16, nq), F32),
            vm((NY, 2, nq, feat), BF16),
            vm((NY, 2, 1, nq), F32),
            vm((NY - 1, 2, nq, feat), BF16),
            vm((NY - 1, 2, 1, nq), F32),
            vm((nk, 2, CAP, feat), BF16),
            vm((nk, 2, CAP, feat), BF16),
            vm((NY, qb, feat), BF16),
            vm((NY - 1, qb, feat), BF16),
            vm((NY, qb, 128), BF16),
            vm((NY, qb, 128), BF16),
            vm((NY, 2 * feat, hid), BF16),
            vm((NY, hid, feat), BF16),
            vm((NY, 8, hid), F32),
            dma((2,)),
            dma((nk,)), dma((nk,)), dma((nk,)), dma((nk,)),
            dma((3,)), dma((3,)), dma((3,)), dma((3,)),
            dma((3, 3)), dma((3, 3)),
            dma((3, 2)), dma((3, 2)), dma((3, 2)), dma((3, 2)),
            dma((nk,)), dma((nk,)),
            dma((3,)), dma((3,)), dma((3,)), dma((3,)),
            dma((2,)),
        ],
        compiler_params=pltpu.CompilerParams(
            collective_id=0, has_side_effects=True, vmem_limit_bytes=56 * 1024 * 1024
        ),
    )(queries, query_owner.reshape(1, qn), probes.T, list_slab, row_owner, proj_in, bias_in.reshape(1, hid), proj_out)


def solution(mesh):
    in_specs = (
        P("list", None),
        P("list"),
        P("list", None),
        P("list", "row", None),
        P("list", "row"),
        P(None, "row"),
        P("row"),
        P("row", None),
    )
    out_specs = P("list", "row")
    return jax.shard_map(body, mesh=mesh, in_specs=in_specs, out_specs=out_specs, check_vma=False)
```

time: 282 us -> 87.2 us (0.31)
  waiting for transfers between devices: 120 us -> 0 us
  Pallas kernels: 0 us -> 83.9 us
  local copies, waits for them, and re-layouts: 36.8 us -> 2.76 us
  starting transfers between devices: 32.4 us -> 0 us
  blocking collectives: 31.6 us -> 0 us
  matrix products: 24.1 us -> 0 us
  other arithmetic: 22.7 us -> 0 us
  between operations: 13.8 us -> 0.01 us
    pallas_call x0 -> x1, Pallas kernels: none -> 83.9 us  [body(): pl.pallas_call(kernel, out_shape=jax.ShapeDtypeStruct((qn, feat // NY), B...]
    all_to_all x3 -> x0, waiting for transfers between devices: 55.2 us -> none  [the longest x1 27.8 us: body(): lax.all_to_all(context, 'list', split_axis=0, concat_axis=0, tiled=True)]
    psum x1 -> x0, waiting for transfers between devices: 44.8 us -> none  [body(): weighted, weight_total = lax.psum((weighted, weight_total), 'row')]
    all_to_all x3 -> x0, starting transfers between devices: 32.4 us -> none  [the longest x1 11.6 us: body(): lax.all_to_all(send_owner, 'list', split_axis=0, concat_axis=0, tiled=True)]
    gather x3 -> x0, local copies, waits for them, and re-layouts: 26.1 us -> none  [the longest x1 13.2 us: body(): send_owner = padded_owner[source].reshape(n_list, lists_here, capacity)]
    dot_general x5 -> x0, matrix products: 24.1 us -> none  [the longest x2 18.2 us: body(): jnp.einsum('qe,re->qr', rows_q, list_slab[list_pos], preferred_element_ty...]
    reduce_scatter x1 -> x0, waiting for transfers between devices: 19.5 us -> none  [body(): lax.psum_scatter(partial_out, 'row', scatter_dimension=1, tiled=True)]
    pmax x1 -> x0, blocking collectives: 17.2 us -> none  [body(): row_peak = lax.pmax(jnp.stack(maxima, axis=1), 'row')]
  transfers between devices with their start and end apart: 5 -> 0, of which waited for: 4 -> 0; matrix products, arithmetic and copies ran while one was open for 4% -> 0% of each run, Pallas kernels for 0% -> 0%
where the time goes in v1:
time: 87.2 us; the launch traced here: 86.7 us
  Pallas kernels  83.9 us (96%)
  local copies, waits for them, and re-layouts  2.76 us (3%)
    pallas_call x1, Pallas kernels, body(): pl.pallas_call(kernel, out_shape=jax.ShapeDtypeStruct((qn, feat // NY), B...  83.9 us

profile of v1, /device:TPU:32, one launch (start us, length us, event | category | flops | bytes accessed | tf_op | source)
XLA Modules:
  0.0 86.7 jit_solution(6525997338060533413)
XLA Ops:
  0.0 1.2 %reshape.7.bias_ref = bf16[1,256]{1,0:T(2,128)(2,1)} reshape(bf16[256]{0:T(256)(128)(2,1)} %param.14) | data formatting | bytes 1024 | tf_op jit(solution)/shard_map/reshape | solution.py:432
  1.2 83.9 %shard_map.82 = bf16[256,64]{1,0:T(8,128)(2,1)} custom-call(bf16[256,256]{1,0:T(8,128)(2,1)} %q_ref.1, s32[1,256]{1,0:T(1,128)} %bitcast.3, s32[4,256]{1,0:T(4,128)} %bitcast.2, bf16[2,4096,256]{2,1,0:T(8,128)(2,1)} %slab_hbm.1, s32[2,4096]{1,0:T(2,128)} %rowner_ref.1, bf16[512,256]{1,0:T(8,128)(2,1)} %win_ref.1, bf16[1,256]{1,0:T(2,128)(2,1)} %reshape.7.bias_ref, ...), custom_call_target="tpu_custom_call" | custom-call | tf_op jit(solution)/shard_map/pallas_call | solution.py:388
  85.1 1.5 %copy.9 = bf16[256,64]{0,1:T(8,128)(2,1)} copy(bf16[256,64]{1,0:T(8,128)(2,1)} %shard_map.82) | data formatting | bytes 65536 | tf_op jit(solution)/shard_map/pallas_call | solution.py:388

commit v2 on v1

--- a/solution.py
+++ b/solution.py
@@ -11,7 +11,7 @@
 LOG2E = math.log2(math.e)
 NX, NZ, NC, NY = 4, 8, 2, 4
 CAP = 16
-TILE = 512
+TILE = 2048
 MESH = pl.DeviceIdType.MESH
 F32 = jnp.float32
 BF16 = jnp.bfloat16
@@ -34,7 +34,7 @@
     slab, kt, rcol, onehot, onehot_t, send_q, send_o, recv_q, recv_o, own_o, qt, scores, acc,
     part, lse, rpart, rlse, ctx, ret, pq, rpq, blk, rblk, wi, wo, bi,
     slab_sem, a2a_s, a2a_r, o_s, o_r, ag_s, ag_r, ago_s, ago_r, w_s, w_r, rs_s, rs_r, rl_s, rl_r,
-    ret_s, ret_r, pq_s, pq_r, blk_s, blk_r, loc_sem,
+    f_s, f_r, ret_s, ret_r, pq_s, pq_r, blk_s, blk_r, loc_sem,
 ):
     nk = NZ * NC
     nq = nk * CAP
@@ -58,6 +58,8 @@
     barrier = pltpu.get_barrier_semaphore()
     for j in (1, 2, 3):
         pl.semaphore_signal(barrier, inc=1, device_id=(li, peer(j)), device_id_type=MESH)
+    sibling = (li + 1 - 2 * core, y)
+    pl.semaphore_signal(barrier, inc=1, device_id=sibling, device_id_type=MESH)
 
     @pl.when(y != 0)
     def _():
@@ -102,7 +104,23 @@
         send_o[i : i + 1, :] = nt_dot(own8, onehot[:, i].reshape(nq, qn))[0:1, :]
     bi[y] = jnp.broadcast_to(bias_ref[...].astype(F32), (8, bias_ref.shape[1]))
 
-    pl.semaphore_wait(barrier, 19 - 16 + nk - (1 - (y + 3) // 4))
+    onehot_t[...] = oh.astype(F32).T.astype(BF16)
+    kt[:, :, feat : feat + 16, :] = jnp.ones((2, ntile, 16, tile), BF16)
+    ptile = min(tile, 512)
+    for l in range(2):
+        slab_copies[l].wait()
+
+        def prep(t, c):
+            rows_t = slab[l, pl.ds(t * ptile, ptile), :]
+            kt[l, t // (tile // ptile), 0:feat, pl.ds(t % (tile // ptile) * ptile, ptile)] = rows_t.astype(F32).T.astype(BF16)
+            for h in range(ptile // 128):
+                rr = rowner_ref[l : l + 1, pl.ds(t * ptile + h * 128, 128)].astype(F32)
+                rcol[l, pl.ds(t * ptile + h * 128, 128), :] = jnp.broadcast_to(rr, (128, 128)).T
+            return c
+
+        lax.fori_loop(0, rows // ptile, prep, 0)
+
+    pl.semaphore_wait(barrier, 4 + nk - (1 - (y + 3) // 4))
 
     def q_copy(k):
         return pltpu.make_async_remote_copy(
@@ -134,74 +152,98 @@
 
     lax.fori_loop(1, nk, a2a_start, 0)
 
+    ih, oh2 = 2 * feat // NC, wo.shape[1] // NC
+    in_half = pl.ds(pl.multiple_of(core * ih, ih), ih)
+    out_half = pl.ds(pl.multiple_of(core * oh2, oh2), oh2)
+
     def w_copies(j):
-        dev = (li, peer(j))
         return [
             pltpu.make_async_remote_copy(
-                src_ref=s, dst_ref=d.at[y], send_sem=w_s.at[n, j - 1], recv_sem=w_r.at[n, j - 1],
-                device_id=dev, device_id_type=MESH)
-            for n, (s, d) in enumerate(((win_ref, wi), (wout_ref, wo), (bi.at[y], bi)))
+                src_ref=s, dst_ref=d, send_sem=w_s.at[n, j - 1], recv_sem=w_r.at[n, j - 1],
+                device_id=(li, peer(j)), device_id_type=MESH)
+            for n, (s, d) in enumerate((
+                (win_ref.at[in_half], wi.at[y, in_half]),
+                (wout_ref.at[out_half], wo.at[y, out_half]),
+                (bi.at[y], bi.at[y])))
         ]
 
-    weight_copies = [c for j in (1, 2, 3) for c in w_copies(j)]
+    def share_copies(j):
+        src = peer(NY - j)
+        return [
+            pltpu.make_async_remote_copy(
+                src_ref=d, dst_ref=d, send_sem=f_s.at[n, j - 1], recv_sem=f_r.at[n, j - 1],
+                device_id=sibling, device_id_type=MESH)
+            for n, d in enumerate((wi.at[src, in_half], wo.at[src, out_half]))
+        ]
+
+    weight_copies = [c for j in (1, 3, 2) for c in w_copies(j)]
     for c in weight_copies:
         c.start()
     local = [pltpu.make_async_copy(win_ref, wi.at[y], loc_sem.at[0]), pltpu.make_async_copy(wout_ref, wo.at[y], loc_sem.at[1])]
     for c in local:
         c.start()
 
-    onehot_t[...] = oh.astype(F32).T.astype(BF16)
-    for l in range(2):
-        slab_copies[l].wait()
-
-        def prep(t, c):
-            blkk = slab[l, pl.ds(t * tile, tile), :]
-            kt[l, t, 0:feat, :] = blkk.astype(F32).T.astype(BF16)
-            kt[l, t, feat : feat + 16, :] = jnp.ones((16, tile), BF16)
-            for h in range(tile // 128):
-                rr = rowner_ref[l : l + 1, pl.ds(t * tile + h * 128, 128)].astype(F32)
-                rcol[l, pl.ds(t * tile + h * 128, 128), :] = jnp.broadcast_to(rr, (128, 128)).T
-            return c
-
-        lax.fori_loop(0, ntile, prep, 0)
+    part_of = (pl.ds(0, nk // 2), pl.ds(nk // 2, nk // 2))
+
+    def near_copy(j, p):
+        return pltpu.make_async_remote_copy(
+            src_ref=recv_q.at[y, part_of[p]], dst_ref=recv_q.at[y, part_of[p]],
+            send_sem=ag_s.at[j - 1, p], recv_sem=ag_r.at[j - 1, p],
+            device_id=(li, peer(j)), device_id_type=MESH)
+
+    def far_copy(p):
+        src, dst = (peer(3), peer(1)) if p == 0 else (peer(1), peer(3))
+        return pltpu.make_async_remote_copy(
+            src_ref=recv_q.at[src, part_of[p]], dst_ref=recv_q.at[src, part_of[p]],
+            send_sem=ag_s.at[1, p], recv_sem=ag_r.at[1, p],
+            device_id=(li, dst), device_id_type=MESH)
+
+    def owners_copy(j):
+        return pltpu.make_async_remote_copy(
+            src_ref=own_o.at[y], dst_ref=own_o.at[y], send_sem=ago_s.at[j - 1], recv_sem=ago_r.at[j - 1],
+            device_id=(li, peer(j)), device_id_type=MESH)
 
     @pl.when(y == 0)
     def _():
         q_self.wait()
-        o_self.wait()
 
     @pl.when(y != 0)
     def _():
         q_copy(0).wait()
-        o_copy(0).wait()
 
     def a2a_wait(k, c):
         q_copy(k).wait()
+        return c
+
+    lax.fori_loop(1, nk // 2, a2a_wait, 0)
+    for j in (1, 3):
+        near_copy(j, 0).start()
+    lax.fori_loop(nk // 2, nk, a2a_wait, 0)
+    for j in (1, 3):
+        near_copy(j, 1).start()
+
+    @pl.when(y == 0)
+    def _():
+        o_self.wait()
+
+    @pl.when(y != 0)
+    def _():
+        o_copy(0).wait()
+
+    def o_wait(k, c):
         o_copy(k).wait()
         return c
 
-    lax.fori_loop(1, nk, a2a_wait, 0)
+    lax.fori_loop(1, nk, o_wait, 0)
     lane_k = lax.broadcasted_iota(jnp.int32, (2, nq), 1) // CAP
     total_o = jnp.zeros((2, nq), F32)
     for k in range(nk):
         total_o = total_o + jnp.where(lane_k == k, recv_o[k], 0.0)
     own_o[y] = total_o - 1.0
-
-    def ag_copies(j):
-        dev = (li, peer(j))
-        return [
-            pltpu.make_async_remote_copy(
-                src_ref=s.at[y], dst_ref=s.at[y], send_sem=ss.at[j - 1], recv_sem=rr.at[j - 1],
-                device_id=dev, device_id_type=MESH)
-            for s, ss, rr in ((recv_q, ag_s, ag_r), (own_o, ago_s, ago_r))
-        ]
-
-    ag = {j: ag_copies(j) for j in (1, 3, 2)}
     for j in (1, 3, 2):
-        for c in ag[j]:
-            c.start()
-
-    order = [(0, 0), (1, 0), (3, 0), (1, 1), (3, 1), (2, 0), (2, 1), (0, 1)]
+        owners_copy(j).start()
+
+    order = [(0, 0), (0, 1), (1, 0), (3, 0), (2, 0), (1, 1), (3, 1), (2, 1)]
     arrived = {0}
     rs_sends = []
 
@@ -239,8 +281,17 @@
             j, l = order[n]
             src = peer(NY - j)
             if j not in arrived:
-                for c in ag[j]:
-                    c.wait_recv()
+                if j == 1:
+                    near_copy(1, 0).wait_recv()
+                    far_copy(0).start()
+                    near_copy(3, 0).wait_recv()
+                    near_copy(3, 1).wait_recv()
+                    far_copy(1).start()
+                    near_copy(1, 1).wait_recv()
+                if j == 2:
+                    far_copy(0).wait_recv()
+                    far_copy(1).wait_recv()
+                owners_copy(j).wait_recv()
                 arrived.add(j)
             src = peer(NY - j)
             qt[n % 2] = recv_q[src, :, l].reshape(nq, feat).astype(F32).T.astype(BF16)
@@ -256,6 +307,12 @@
                 m = score_tile(n, order[n][1], t, own_row, m)
             return m
 
+        if n == len(order) - 1:
+            for c in weight_copies:
+                c.wait()
+            for j in (1, 2, 3):
+                for c in share_copies(j):
+                    c.start()
         m = lax.fori_loop(0, ntile, stage, jnp.full((8, nq), -jnp.inf, F32))
         if n > 0:
             pj, pl_ = order[n - 1]
@@ -270,6 +327,14 @@
                     rs_sends.append(c)
         if n < len(order):
             peak = jnp.max(m, axis=0, keepdims=True)
+
+    def ret_copy(k, l):
+        return pltpu.make_async_remote_copy(
+            src_ref=ctx.at[k, l], dst_ref=ret.at[k, l], send_sem=ret_s.at[k, l], recv_sem=ret_r.at[k, l],
+            device_id=(partner(k), y), device_id_type=MESH)
+
+    def ret_self(l):
+        return pltpu.make_async_copy(ctx.at[0, l], ret.at[0, l], ret_r.at[0, l])
 
     for l in range(2):
         for j in (1, 3, 2):
@@ -288,40 +353,35 @@
                 val = val + cols[a] * srcs[a][:, cs].astype(F32)
             ctx[:, l, :, cs] = val.astype(BF16).reshape(nk, CAP, 128)
 
-    def ret_copy(k):
-        return pltpu.make_async_remote_copy(
-            src_ref=ctx.at[k], dst_ref=ret.at[k], send_sem=ret_s.at[k], recv_sem=ret_r.at[k],
-            device_id=(partner(k), y), device_id_type=MESH)
-
-    ret_self = pltpu.make_async_copy(ctx.at[0], ret.at[0], ret_r.at[0])
-
-    @pl.when(y == 0)
-    def _():
-        ret_self.start()
-
-    @pl.when(y != 0)
-    def _():
-        ret_copy(0).start()
-
-    def ret_start(k, c):
-        ret_copy(k).start()
-        return c
-
-    lax.fori_loop(1, nk, ret_start, 0)
-
-    @pl.when(y == 0)
-    def _():
-        ret_self.wait()
-
-    @pl.when(y != 0)
-    def _():
-        ret_copy(0).wait()
-
-    def ret_wait(k, c):
-        ret_copy(k).wait()
-        return c
-
-    lax.fori_loop(1, nk, ret_wait, 0)
+        @pl.when(y == 0)
+        def _(l=l):
+            ret_self(l).start()
+
+        @pl.when(y != 0)
+        def _(l=l):
+            ret_copy(0, l).start()
+
+        def ret_start(k, c, l=l):
+            ret_copy(k, l).start()
+            return c
+
+        lax.fori_loop(1, nk, ret_start, 0)
+
+    for l in range(2):
+
+        @pl.when(y == 0)
+        def _(l=l):
+            ret_self(l).wait()
+
+        @pl.when(y != 0)
+        def _(l=l):
+            ret_copy(0, l).wait()
+
+        def ret_wait(k, c, l=l):
+            ret_copy(k, l).wait()
+            return c
+
+        lax.fori_loop(1, nk, ret_wait, 0)
 
     share = jnp.dot(onehot_t[...], ret[...].reshape(nl * CAP, feat), preferred_element_type=F32) * 0.25
     qb = qn // NY
@@ -332,8 +392,9 @@
             src_ref=pq.at[peer(j)], dst_ref=rpq.at[j - 1], send_sem=pq_s.at[j - 1], recv_sem=pq_r.at[j - 1],
             device_id=(li, peer(j)), device_id_type=MESH)
         pq_copies[j].start()
-    for c in weight_copies:
-        c.wait()
+    for j in (1, 2, 3):
+        for c in share_copies(j):
+            c.wait()
     for c in local:
         c.wait()
     mine = q_ref[pl.ds(pl.multiple_of(y * qb, qb), qb), :]
@@ -361,9 +422,12 @@
             device_id=(li, peer(j)), device_id_type=MESH)
         blk_copies[j].start()
     out_ref[pl.ds(pl.multiple_of(y * qb, qb), qb), :] = blk[y][:, 0:ob]
-    for j in (1, 2, 3):
-        for c in ag[j]:
-            c.wait_send()
+    for p in range(2):
+        for j in (1, 3):
+            near_copy(j, p).wait_send()
+        far_copy(p).wait_send()
+    for j in (1, 2, 3):
+        owners_copy(j).wait_send()
     for c in rs_sends:
         c.wait_send()
     for j in (1, 2, 3):
@@ -419,10 +483,10 @@
             vm((NY, 8, hid), F32),
             dma((2,)),
             dma((nk,)), dma((nk,)), dma((nk,)), dma((nk,)),
-            dma((3,)), dma((3,)), dma((3,)), dma((3,)),
+            dma((3, 2)), dma((3, 2)), dma((3,)), dma((3,)),
             dma((3, 3)), dma((3, 3)),
             dma((3, 2)), dma((3, 2)), dma((3, 2)), dma((3, 2)),
-            dma((nk,)), dma((nk,)),
+            dma((2, 3)), dma((2, 3)), dma((nk, 2)), dma((nk, 2)),
             dma((3,)), dma((3,)), dma((3,)), dma((3,)),
             dma((2,)),
         ],

time: 87.2 us -> 71.2 us (0.82)
  Pallas kernels: 83.9 us -> 68.3 us
    pallas_call x1, Pallas kernels: 83.9 us -> 68.3 us  [body(): pl.pallas_call(kernel, out_shape=jax.ShapeDtypeStruct((qn, feat // NY), B...]
where the time goes in v2:
time: 71.2 us; the launch traced here: 71 us
  Pallas kernels  68.3 us (96%)
  local copies, waits for them, and re-layouts  2.76 us (4%)
    pallas_call x1, Pallas kernels, body(): pl.pallas_call(kernel, out_shape=jax.ShapeDtypeStruct((qn, feat // NY), B...  68.3 us
    pallas_call x1, local copies, waits for them, and re-layouts, body(): pl.pallas_call(kernel, out_shape=jax.ShapeDtypeStruct((qn, feat // NY), B...  1.54 us

profile of v2, /device:TPU:32, one launch (start us, length us, event | category | flops | bytes accessed | tf_op | source)
XLA Modules:
  0.0 71.0 jit_solution(3733123683627991579)
XLA Ops:
  0.0 1.2 %reshape.7.bias_ref = bf16[1,256]{1,0:T(2,128)(2,1)} reshape(bf16[256]{0:T(256)(128)(2,1)} %param.14) | data formatting | bytes 1024 | tf_op jit(solution)/shard_map/reshape | solution.py:496
  1.2 68.3 %shard_map.82 = bf16[256,64]{1,0:T(8,128)(2,1)} custom-call(bf16[256,256]{1,0:T(8,128)(2,1)} %q_ref.1, s32[1,256]{1,0:T(1,128)} %bitcast.3, s32[4,256]{1,0:T(4,128)} %bitcast.2, bf16[2,4096,256]{2,1,0:T(8,128)(2,1)} %slab_hbm.1, s32[2,4096]{1,0:T(2,128)} %rowner_ref.1, bf16[512,256]{1,0:T(8,128)(2,1)} %win_ref.1, bf16[1,256]{1,0:T(2,128)(2,1)} %reshape.7.bias_ref, ...), custom_call_target="tpu_custom_call" | custom-call | tf_op jit(solution)/shard_map/pallas_call | solution.py:452
  69.5 1.5 %copy.9 = bf16[256,64]{0,1:T(8,128)(2,1)} copy(bf16[256,64]{1,0:T(8,128)(2,1)} %shard_map.82) | data formatting | bytes 65536 | tf_op jit(solution)/shard_map/pallas_call | solution.py:452

commit v3 on v2

--- a/solution.py
+++ b/solution.py
@@ -29,9 +29,9 @@
 
 
 def kernel(
-    q_ref, owner_ref, probes_ref, slab_hbm, rowner_ref, win_ref, bias_ref, wout_ref,
+    q_ref, owner_ref, probes_ref, slab_hbm, rowner_hbm, win_ref, bias_ref, wout_ref,
     out_ref,
-    slab, kt, rcol, onehot, onehot_t, send_q, send_o, recv_q, recv_o, own_o, qt, scores, acc,
+    slab, rowner_ref, kt, rcol, onehot, onehot_t, send_q, send_o, recv_q, recv_o, own_o, qt, scores, acc,
     part, lse, rpart, rlse, ctx, ret, pq, rpq, blk, rblk, wi, wo, bi,
     slab_sem, a2a_s, a2a_r, o_s, o_r, ag_s, ag_r, ago_s, ago_r, w_s, w_r, rs_s, rs_r, rl_s, rl_r,
     f_s, f_r, ret_s, ret_r, pq_s, pq_r, blk_s, blk_r, loc_sem,
@@ -72,6 +72,7 @@
     lax.fori_loop(1, nk, sig, 0)
 
     slab_copies = [pltpu.make_async_copy(slab_hbm.at[l], slab.at[l], slab_sem.at[l]) for l in range(2)]
+    slab_copies.append(pltpu.make_async_copy(rowner_hbm, rowner_ref, slab_sem.at[2]))
     for c in slab_copies:
         c.start()
 
@@ -96,30 +97,12 @@
     slot = lax.broadcasted_iota(jnp.int32, (CAP, qn), 0).astype(F32)
     for r in range(nl):
         onehot[r // 2, r % 2] = jnp.where(rank[r : r + 1, :] == slot, 1.0, 0.0).astype(BF16)
-    oh = onehot[...].reshape(nl * CAP, qn)
-    picked = jnp.dot(oh, q_ref[...], preferred_element_type=F32) * (1.0 / math.sqrt(feat))
-    send_q[...] = picked.astype(BF16).reshape(send_q.shape)
-    own8 = jnp.broadcast_to((owner_ref[...] + 1).astype(F32), (8, qn)).astype(BF16)
-    for i in range(2):
-        send_o[i : i + 1, :] = nt_dot(own8, onehot[:, i].reshape(nq, qn))[0:1, :]
-    bi[y] = jnp.broadcast_to(bias_ref[...].astype(F32), (8, bias_ref.shape[1]))
-
-    onehot_t[...] = oh.astype(F32).T.astype(BF16)
-    kt[:, :, feat : feat + 16, :] = jnp.ones((2, ntile, 16, tile), BF16)
-    ptile = min(tile, 512)
-    for l in range(2):
-        slab_copies[l].wait()
-
-        def prep(t, c):
-            rows_t = slab[l, pl.ds(t * ptile, ptile), :]
-            kt[l, t // (tile // ptile), 0:feat, pl.ds(t % (tile // ptile) * ptile, ptile)] = rows_t.astype(F32).T.astype(BF16)
-            for h in range(ptile // 128):
-                rr = rowner_ref[l : l + 1, pl.ds(t * ptile + h * 128, 128)].astype(F32)
-                rcol[l, pl.ds(t * ptile + h * 128, 128), :] = jnp.broadcast_to(rr, (128, 128)).T
-            return c
-
-        lax.fori_loop(0, rows // ptile, prep, 0)
-
+    def pick(p):
+        half = onehot[p * nk // 2 : (p + 1) * nk // 2].reshape(nq, qn)
+        picked = jnp.dot(half, q_ref[...], preferred_element_type=F32) * (1.0 / math.sqrt(feat))
+        send_q[p * nk // 2 : (p + 1) * nk // 2] = picked.astype(BF16).reshape(nk // 2, 2, CAP, feat)
+
+    pick(0)
     pl.semaphore_wait(barrier, 4 + nk - (1 - (y + 3) // 4))
 
     def q_copy(k):
@@ -138,19 +121,37 @@
     @pl.when(y == 0)
     def _():
         q_self.start()
-        o_self.start()
 
     @pl.when(y != 0)
     def _():
         q_copy(0).start()
-        o_copy(0).start()
-
-    def a2a_start(k, c):
+
+    def q_start(k, c):
         q_copy(k).start()
+        return c
+
+    def o_start(k, c):
         o_copy(k).start()
         return c
 
-    lax.fori_loop(1, nk, a2a_start, 0)
+    lax.fori_loop(1, nk // 2, q_start, 0)
+    pick(1)
+    lax.fori_loop(nk // 2, nk, q_start, 0)
+    own8 = jnp.broadcast_to((owner_ref[...] + 1).astype(F32), (8, qn)).astype(BF16)
+    for i in range(2):
+        send_o[i : i + 1, :] = nt_dot(own8, onehot[:, i].reshape(nq, qn))[0:1, :]
+    bi[y] = jnp.broadcast_to(bias_ref[...].astype(F32).reshape(1, bias_ref.shape[0]), (8, bias_ref.shape[0]))
+
+
+    @pl.when(y == 0)
+    def _():
+        o_self.start()
+
+    @pl.when(y != 0)
+    def _():
+        o_copy(0).start()
+
+    lax.fori_loop(1, nk, o_start, 0)
 
     ih, oh2 = 2 * feat // NC, wo.shape[1] // NC
     in_half = pl.ds(pl.multiple_of(core * ih, ih), ih)
@@ -176,12 +177,30 @@
             for n, d in enumerate((wi.at[src, in_half], wo.at[src, out_half]))
         ]
 
-    weight_copies = [c for j in (1, 3, 2) for c in w_copies(j)]
-    for c in weight_copies:
-        c.start()
+    weight_copies = {j: w_copies(j) for j in (1, 3, 2)}
+    for j in (1, 3, 2):
+        for c in weight_copies[j][1:]:
+            c.start()
     local = [pltpu.make_async_copy(win_ref, wi.at[y], loc_sem.at[0]), pltpu.make_async_copy(wout_ref, wo.at[y], loc_sem.at[1])]
     for c in local:
         c.start()
+
+    onehot_t[...] = onehot[...].reshape(nl * CAP, qn).astype(F32).T.astype(BF16)
+    kt[:, :, feat : feat + 16, :] = jnp.ones((2, ntile, 16, tile), BF16)
+    ptile = min(tile, 512)
+    slab_copies[2].wait()
+    for l in range(2):
+        slab_copies[l].wait()
+
+        def prep(t, c):
+            rows_t = slab[l, pl.ds(t * ptile, ptile), :]
+            kt[l, t // (tile // ptile), 0:feat, pl.ds(t % (tile // ptile) * ptile, ptile)] = rows_t.astype(F32).T.astype(BF16)
+            for h in range(ptile // 128):
+                rr = rowner_ref[l : l + 1, pl.ds(t * ptile + h * 128, 128)].astype(F32)
+                rcol[l, pl.ds(t * ptile + h * 128, 128), :] = jnp.broadcast_to(rr, (128, 128)).T
+            return c
+
+        lax.fori_loop(0, rows // ptile, prep, 0)
 
     part_of = (pl.ds(0, nk // 2), pl.ds(nk // 2, nk // 2))
 
@@ -243,7 +262,7 @@
     for j in (1, 3, 2):
         owners_copy(j).start()
 
-    order = [(0, 0), (0, 1), (1, 0), (3, 0), (2, 0), (1, 1), (3, 1), (2, 1)]
+    order = [(0, 0), (0, 1), (1, 0), (3, 0), (1, 1), (2, 0), (2, 1), (3, 1)]
     arrived = {0}
     rs_sends = []
 
@@ -307,12 +326,6 @@
                 m = score_tile(n, order[n][1], t, own_row, m)
             return m
 
-        if n == len(order) - 1:
-            for c in weight_copies:
-                c.wait()
-            for j in (1, 2, 3):
-                for c in share_copies(j):
-                    c.start()
         m = lax.fori_loop(0, ntile, stage, jnp.full((8, nq), -jnp.inf, F32))
         if n > 0:
             pj, pl_ = order[n - 1]
@@ -327,6 +340,9 @@
                     rs_sends.append(c)
         if n < len(order):
             peak = jnp.max(m, axis=0, keepdims=True)
+
+    for j in (1, 3, 2):
+        weight_copies[j][0].start()
 
     def ret_copy(k, l):
         return pltpu.make_async_remote_copy(
@@ -392,7 +408,12 @@
             src_ref=pq.at[peer(j)], dst_ref=rpq.at[j - 1], send_sem=pq_s.at[j - 1], recv_sem=pq_r.at[j - 1],
             device_id=(li, peer(j)), device_id_type=MESH)
         pq_copies[j].start()
-    for j in (1, 2, 3):
+    for j in (1, 3, 2):
+        for c in weight_copies[j]:
+            c.wait()
+        for c in share_copies(j):
+            c.start()
+    for j in (1, 3, 2):
         for c in share_copies(j):
             c.wait()
     for c in local:
@@ -421,7 +442,7 @@
             src_ref=blk.at[peer(j)], dst_ref=rblk.at[y], send_sem=blk_s.at[j - 1], recv_sem=blk_r.at[j - 1],
             device_id=(li, peer(j)), device_id_type=MESH)
         blk_copies[j].start()
-    out_ref[pl.ds(pl.multiple_of(y * qb, qb), qb), :] = blk[y][:, 0:ob]
+    rblk[y] = blk[y]
     for p in range(2):
         for j in (1, 3):
             near_copy(j, p).wait_send()
@@ -432,8 +453,8 @@
         c.wait_send()
     for j in (1, 2, 3):
         blk_copies[j].wait()
-        src = peer(NY - j)
-        out_ref[pl.ds(pl.multiple_of(src * qb, qb), qb), :] = rblk[src][:, 0:ob]
+    full = rblk[...].reshape(qn, 128).astype(F32)
+    out_ref[...] = full.T[0:ob, :].astype(BF16)
 
 
 def body(queries, query_owner, probes, list_slab, row_owner, proj_in, bias_in, proj_out):
@@ -449,13 +470,15 @@
     vm = pltpu.VMEM
     dma = pltpu.SemaphoreType.DMA
     vspec = pl.BlockSpec(memory_space=pltpu.VMEM)
-    return pl.pallas_call(
+    hbm = pl.BlockSpec(memory_space=pl.ANY)
+    out_t = pl.pallas_call(
         kernel,
-        out_shape=jax.ShapeDtypeStruct((qn, feat // NY), BF16),
-        in_specs=[vspec, vspec, vspec, pl.BlockSpec(memory_space=pl.ANY), vspec, vspec, vspec, vspec],
+        out_shape=jax.ShapeDtypeStruct((feat // NY, qn), BF16),
+        in_specs=[vspec, vspec, vspec, hbm, hbm, hbm, vspec, hbm],
         out_specs=vspec,
         scratch_shapes=[
             vm((lists, rows, feat), BF16),
+            vm((lists, rows), jnp.int32),
             vm((lists, nt, feat + 16, tile), BF16),
             vm((lists, rows, 128), F32),
             vm((nk, 2, CAP, qn), BF16),
@@ -481,7 +504,7 @@
             vm((NY, 2 * feat, hid), BF16),
             vm((NY, hid, feat), BF16),
             vm((NY, 8, hid), F32),
-            dma((2,)),
+            dma((3,)),
             dma((nk,)), dma((nk,)), dma((nk,)), dma((nk,)),
             dma((3, 2)), dma((3, 2)), dma((3,)), dma((3,)),
             dma((3, 3)), dma((3, 3)),
@@ -493,7 +516,8 @@
         compiler_params=pltpu.CompilerParams(
             collective_id=0, has_side_effects=True, vmem_limit_bytes=56 * 1024 * 1024
         ),
-    )(queries, query_owner.reshape(1, qn), probes.T, list_slab, row_owner, proj_in, bias_in.reshape(1, hid), proj_out)
+    )(queries, query_owner.reshape(1, qn), probes.T, list_slab, row_owner, proj_in, bias_in, proj_out)
+    return out_t.T
 
 
 def solution(mesh):

time: 71.2 us -> 66.6 us (0.935); the launches traced: 71 us -> 65.6 us
  Pallas kernels: 68.3 us -> 64.2 us
  local copies, waits for them, and re-layouts: 2.76 us -> 1.38 us
    pallas_call x1, Pallas kernels: 68.3 us -> 64.2 us  [body(): pl.pallas_call(kernel, out_shape=jax.ShapeDtypeStruct((feat // NY, qn), B...]
    pallas_call x1 -> x0, local copies, waits for them, and re-layouts: 1.54 us -> none  [body(): pl.pallas_call(kernel, out_shape=jax.ShapeDtypeStruct((qn, feat // NY), B...]
    unnamed x0 -> x1, local copies, waits for them, and re-layouts: none -> 1.38 us
    reshape x1 -> x0, local copies, waits for them, and re-layouts: 1.22 us -> none  [body(): bias_in.reshape(1, hid)]
where the time goes in v3:
time: 66.6 us; the launch traced here: 65.6 us
  Pallas kernels  64.2 us (96%)
  local copies, waits for them, and re-layouts  1.38 us (2%)
    pallas_call x1, Pallas kernels, body(): pl.pallas_call(kernel, out_shape=jax.ShapeDtypeStruct((feat // NY, qn), B...  64.2 us
    unnamed x1, local copies, waits for them, and re-layouts  1.38 us

profile of v3, /device:TPU:32, one launch (start us, length us, event | category | flops | bytes accessed | tf_op | source)
XLA Modules:
  0.0 65.6 jit_solution(4865685353806187288)
XLA Ops:
  0.0 64.2 %shard_map.82 = bf16[64,256]{1,0:T(8,128)(2,1)} custom-call(bf16[256,256]{1,0:T(8,128)(2,1)} %q_ref.1, s32[1,256]{1,0:T(1,128)} %bitcast.5, s32[4,256]{1,0:T(4,128)} %bitcast.4, bf16[2,4096,256]{2,1,0:T(8,128)(2,1)} %slab_hbm.1, s32[2,4096]{1,0:T(2,128)} %rowner_hbm.1, bf16[512,256]{1,0:T(8,128)(2,1)} %win_ref.1, bf16[256]{0:T(256)(128)(2,1)} %bias_ref.1, ...), custom_call_target="tpu_custom_call" | custom-call | tf_op jit(solution)/shard_map/pallas_call | solution.py:474
  64.2 1.4 %copy.10 = bf16[256,64]{0,1:T(8,128)(2,1)} copy(bf16[256,64]{0,1:T(8,128)(2,1)} %bitcast.3) | data formatting | bytes 65536

commit v4 on v3

--- a/solution.py
+++ b/solution.py
@@ -78,12 +78,12 @@
 
     nl = 2 * nk
     row = lax.broadcasted_iota(jnp.int32, (nl, q_ref.shape[0]), 0)
-    kk = row // 2
+    kk = row % nk
     dz = kk // NC
     xd = x ^ y ^ (dz & 3)
     zd = z ^ dz
     cd = (core + kk) % NC
-    lvec = ((xd * NZ + zd) * NC + cd) * 2 + row % 2
+    lvec = ((xd * NZ + zd) * NC + cd) * 2 + row // nk
     hit = probes_ref[0:1, :] == lvec
     for j in range(1, 4):
         hit = hit | (probes_ref[j : j + 1, :] == lvec)
@@ -96,18 +96,21 @@
     rank = jnp.where(hit, rank, -1.0)
     slot = lax.broadcasted_iota(jnp.int32, (CAP, qn), 0).astype(F32)
     for r in range(nl):
-        onehot[r // 2, r % 2] = jnp.where(rank[r : r + 1, :] == slot, 1.0, 0.0).astype(BF16)
-    def pick(p):
-        half = onehot[p * nk // 2 : (p + 1) * nk // 2].reshape(nq, qn)
-        picked = jnp.dot(half, q_ref[...], preferred_element_type=F32) * (1.0 / math.sqrt(feat))
-        send_q[p * nk // 2 : (p + 1) * nk // 2] = picked.astype(BF16).reshape(nk // 2, 2, CAP, feat)
+        onehot[r // nk, r % nk] = jnp.where(rank[r : r + 1, :] == slot, 1.0, 0.0).astype(BF16)
+    def pick(l):
+        picked = jnp.dot(onehot[l].reshape(nq, qn), q_ref[...], preferred_element_type=F32) * (1.0 / math.sqrt(feat))
+        send_q[l] = picked.astype(BF16).reshape(nk, CAP, feat)
 
     pick(0)
+    own8 = jnp.broadcast_to((owner_ref[...] + 1).astype(F32), (8, qn)).astype(BF16)
+    for i in range(2):
+        send_o[i : i + 1, :] = nt_dot(own8, onehot[i].reshape(nq, qn))[0:1, :]
+
     pl.semaphore_wait(barrier, 4 + nk - (1 - (y + 3) // 4))
 
-    def q_copy(k):
-        return pltpu.make_async_remote_copy(
-            src_ref=send_q.at[k], dst_ref=recv_q.at[y, k], send_sem=a2a_s.at[k], recv_sem=a2a_r.at[k],
+    def q_copy(k, l):
+        return pltpu.make_async_remote_copy(
+            src_ref=send_q.at[l, k], dst_ref=recv_q.at[y, l, k], send_sem=a2a_s.at[l, k], recv_sem=a2a_r.at[l, k],
             device_id=(partner(k), y), device_id_type=MESH)
 
     def o_copy(k):
@@ -115,43 +118,29 @@
             src_ref=send_o, dst_ref=recv_o.at[k], send_sem=o_s.at[k], recv_sem=o_r.at[k],
             device_id=(partner(k), y), device_id_type=MESH)
 
-    q_self = pltpu.make_async_copy(send_q.at[0], recv_q.at[y, 0], a2a_r.at[0])
+    q_self = [pltpu.make_async_copy(send_q.at[l, 0], recv_q.at[y, l, 0], a2a_r.at[l, 0]) for l in range(2)]
     o_self = pltpu.make_async_copy(send_o, recv_o.at[0], o_r.at[0])
 
-    @pl.when(y == 0)
-    def _():
-        q_self.start()
-
-    @pl.when(y != 0)
-    def _():
-        q_copy(0).start()
-
-    def q_start(k, c):
-        q_copy(k).start()
-        return c
-
-    def o_start(k, c):
-        o_copy(k).start()
-        return c
-
-    lax.fori_loop(1, nk // 2, q_start, 0)
+    def all_partners(alone, copy):
+        @pl.when(y == 0)
+        def _():
+            alone()
+
+        @pl.when(y != 0)
+        def _():
+            copy(0)
+
+        def step(k, c):
+            copy(k)
+            return c
+
+        lax.fori_loop(1, nk, step, 0)
+
+    all_partners(q_self[0].start, lambda k: q_copy(k, 0).start())
+    all_partners(o_self.start, lambda k: o_copy(k).start())
     pick(1)
-    lax.fori_loop(nk // 2, nk, q_start, 0)
-    own8 = jnp.broadcast_to((owner_ref[...] + 1).astype(F32), (8, qn)).astype(BF16)
-    for i in range(2):
-        send_o[i : i + 1, :] = nt_dot(own8, onehot[:, i].reshape(nq, qn))[0:1, :]
+    all_partners(q_self[1].start, lambda k: q_copy(k, 1).start())
     bi[y] = jnp.broadcast_to(bias_ref[...].astype(F32).reshape(1, bias_ref.shape[0]), (8, bias_ref.shape[0]))
-
-
-    @pl.when(y == 0)
-    def _():
-        o_self.start()
-
-    @pl.when(y != 0)
-    def _():
-        o_copy(0).start()
-
-    lax.fori_loop(1, nk, o_start, 0)
 
     ih, oh2 = 2 * feat // NC, wo.shape[1] // NC
     in_half = pl.ds(pl.multiple_of(core * ih, ih), ih)
@@ -202,19 +191,19 @@
 
         lax.fori_loop(0, rows // ptile, prep, 0)
 
-    part_of = (pl.ds(0, nk // 2), pl.ds(nk // 2, nk // 2))
-
-    def near_copy(j, p):
-        return pltpu.make_async_remote_copy(
-            src_ref=recv_q.at[y, part_of[p]], dst_ref=recv_q.at[y, part_of[p]],
-            send_sem=ag_s.at[j - 1, p], recv_sem=ag_r.at[j - 1, p],
+    half_of = (pl.ds(0, nk // 2), pl.ds(nk // 2, nk // 2))
+
+    def near_copy(j, l):
+        return pltpu.make_async_remote_copy(
+            src_ref=recv_q.at[y, l], dst_ref=recv_q.at[y, l],
+            send_sem=ag_s.at[j - 1, l, 0], recv_sem=ag_r.at[j - 1, l, 0],
             device_id=(li, peer(j)), device_id_type=MESH)
 
-    def far_copy(p):
+    def far_copy(p, l):
         src, dst = (peer(3), peer(1)) if p == 0 else (peer(1), peer(3))
         return pltpu.make_async_remote_copy(
-            src_ref=recv_q.at[src, part_of[p]], dst_ref=recv_q.at[src, part_of[p]],
-            send_sem=ag_s.at[1, p], recv_sem=ag_r.at[1, p],
+            src_ref=recv_q.at[src, l, half_of[p]], dst_ref=recv_q.at[src, l, half_of[p]],
+            send_sem=ag_s.at[1, l, p], recv_sem=ag_r.at[1, l, p],
             device_id=(li, dst), device_id_type=MESH)
 
     def owners_copy(j):
@@ -222,60 +211,46 @@
             src_ref=own_o.at[y], dst_ref=own_o.at[y], send_sem=ago_s.at[j - 1], recv_sem=ago_r.at[j - 1],
             device_id=(li, peer(j)), device_id_type=MESH)
 
-    @pl.when(y == 0)
-    def _():
-        q_self.wait()
-
-    @pl.when(y != 0)
-    def _():
-        q_copy(0).wait()
-
-    def a2a_wait(k, c):
-        q_copy(k).wait()
-        return c
-
-    lax.fori_loop(1, nk // 2, a2a_wait, 0)
-    for j in (1, 3):
-        near_copy(j, 0).start()
-    lax.fori_loop(nk // 2, nk, a2a_wait, 0)
-    for j in (1, 3):
-        near_copy(j, 1).start()
-
-    @pl.when(y == 0)
-    def _():
-        o_self.wait()
-
-    @pl.when(y != 0)
-    def _():
-        o_copy(0).wait()
-
-    def o_wait(k, c):
-        o_copy(k).wait()
-        return c
-
-    lax.fori_loop(1, nk, o_wait, 0)
-    lane_k = lax.broadcasted_iota(jnp.int32, (2, nq), 1) // CAP
-    total_o = jnp.zeros((2, nq), F32)
-    for k in range(nk):
-        total_o = total_o + jnp.where(lane_k == k, recv_o[k], 0.0)
-    own_o[y] = total_o - 1.0
-    for j in (1, 3, 2):
-        owners_copy(j).start()
-
-    order = [(0, 0), (0, 1), (1, 0), (3, 0), (1, 1), (2, 0), (2, 1), (3, 1)]
-    arrived = {0}
+    def gather(j, l):
+        if j == 0:
+            all_partners(q_self[l].wait, lambda k: q_copy(k, l).wait())
+            for d in (1, 3):
+                near_copy(d, l).start()
+            if l == 0:
+                all_partners(o_self.wait, lambda k: o_copy(k).wait())
+                lane_k = lax.broadcasted_iota(jnp.int32, (2, nq), 1) // CAP
+                total_o = jnp.zeros((2, nq), F32)
+                for k in range(nk):
+                    total_o = total_o + jnp.where(lane_k == k, recv_o[k], 0.0)
+                own_o[y] = total_o - 1.0
+                for d in (1, 3, 2):
+                    owners_copy(d).start()
+        elif j == 1:
+            near_copy(1, l).wait_recv()
+            far_copy(0, l).start()
+            near_copy(3, l).wait_recv()
+            far_copy(1, l).start()
+        elif j == 2:
+            far_copy(0, l).wait_recv()
+            far_copy(1, l).wait_recv()
+        if j != 0 and l == 0:
+            owners_copy(j).wait_recv()
+
+    order = [(0, 0), (0, 1), (1, 0), (3, 0), (1, 1), (2, 0), (3, 1), (2, 1)]
     rs_sends = []
 
-    def rs_copies(j, l):
-        dev = (li, peer(j))
-        return [
-            pltpu.make_async_remote_copy(
-                src_ref=part.at[peer(j), l], dst_ref=rpart.at[j - 1, l], send_sem=rs_s.at[j - 1, l],
-                recv_sem=rs_r.at[j - 1, l], device_id=dev, device_id_type=MESH),
-            pltpu.make_async_remote_copy(
-                src_ref=lse.at[peer(j), l], dst_ref=rlse.at[j - 1, l], send_sem=rl_s.at[j - 1, l],
-                recv_sem=rl_r.at[j - 1, l], device_id=dev, device_id_type=MESH),
-        ]
+    rows_of = (pl.ds(0, nq // 2), pl.ds(nq // 2, nq // 2))
+
+    def rs_copy(j, l, p):
+        return pltpu.make_async_remote_copy(
+            src_ref=part.at[peer(j), l, rows_of[p]], dst_ref=rpart.at[j - 1, l, rows_of[p]],
+            send_sem=rs_s.at[j - 1, l, p], recv_sem=rs_r.at[j - 1, l, p],
+            device_id=(li, peer(j)), device_id_type=MESH)
+
+    def rl_copy(j, l):
+        return pltpu.make_async_remote_copy(
+            src_ref=lse.at[peer(j), l], dst_ref=rlse.at[j - 1, l], send_sem=rl_s.at[j - 1, l],
+            recv_sem=rl_r.at[j - 1, l], device_id=(li, peer(j)), device_id_type=MESH)
 
     def score_tile(n, l, t, own_row, m):
         s = jnp.dot(slab[l, pl.ds(t * tile, tile), :], qt[n % 2], preferred_element_type=F32)
@@ -299,21 +274,9 @@
         if n < len(order):
             j, l = order[n]
             src = peer(NY - j)
-            if j not in arrived:
-                if j == 1:
-                    near_copy(1, 0).wait_recv()
-                    far_copy(0).start()
-                    near_copy(3, 0).wait_recv()
-                    near_copy(3, 1).wait_recv()
-                    far_copy(1).start()
-                    near_copy(1, 1).wait_recv()
-                if j == 2:
-                    far_copy(0).wait_recv()
-                    far_copy(1).wait_recv()
-                owners_copy(j).wait_recv()
-                arrived.add(j)
+            gather(j, l)
             src = peer(NY - j)
-            qt[n % 2] = recv_q[src, :, l].reshape(nq, feat).astype(F32).T.astype(BF16)
+            qt[n % 2] = recv_q[src, l].reshape(nq, feat).astype(F32).T.astype(BF16)
             own_row = own_o[src, l : l + 1, :]
         if n > 0:
             acc[...] = jnp.zeros_like(acc)
@@ -335,7 +298,7 @@
             part[psrc, pl_] = mean.T.astype(BF16)
             lse[psrc, pl_] = prev_peak + jnp.log(total)
             if pj != 0:
-                for c in rs_copies(NY - pj, pl_):
+                for c in (rl_copy(NY - pj, pl_), rs_copy(NY - pj, pl_, 0), rs_copy(NY - pj, pl_, 1)):
                     c.start()
                     rs_sends.append(c)
         if n < len(order):
@@ -346,60 +309,58 @@
 
     def ret_copy(k, l):
         return pltpu.make_async_remote_copy(
-            src_ref=ctx.at[k, l], dst_ref=ret.at[k, l], send_sem=ret_s.at[k, l], recv_sem=ret_r.at[k, l],
+            src_ref=ctx.at[l, k], dst_ref=ret.at[l, k], send_sem=ret_s.at[l, k], recv_sem=ret_r.at[l, k],
             device_id=(partner(k), y), device_id_type=MESH)
 
     def ret_self(l):
-        return pltpu.make_async_copy(ctx.at[0, l], ret.at[0, l], ret_r.at[0, l])
+        return pltpu.make_async_copy(ctx.at[l, 0], ret.at[l, 0], ret_r.at[l, 0])
+
+    def part_partners(p, alone, copy):
+        if p == 0:
+
+            @pl.when(y == 0)
+            def _():
+                alone()
+
+            @pl.when(y != 0)
+            def _():
+                copy(0)
+
+        def step(k, c):
+            copy(k)
+            return c
+
+        lax.fori_loop(max(1, p * nk // 2), (p + 1) * nk // 2, step, 0)
 
     for l in range(2):
         for j in (1, 3, 2):
-            for c in rs_copies(j, l):
-                c.wait_recv()
+            rl_copy(j, l).wait_recv()
         ls = [lse[y, l]] + [rlse[j - 1, l] for j in (1, 2, 3)]
         top = jnp.maximum(jnp.maximum(ls[0], ls[1]), jnp.maximum(ls[2], ls[3]))
         es = [jnp.exp(v - top) for v in ls]
         inv = 1.0 / (es[0] + es[1] + es[2] + es[3])
         cols = [jnp.broadcast_to(e * inv, (128, nq)).T for e in es]
-        srcs = [part[y, l]] + [rpart[j - 1, l] for j in (1, 2, 3)]
-        for h in range(feat // 128):
-            cs = slice(h * 128, (h + 1) * 128)
-            val = cols[0] * srcs[0][:, cs].astype(F32)
-            for a in range(1, 4):
-                val = val + cols[a] * srcs[a][:, cs].astype(F32)
-            ctx[:, l, :, cs] = val.astype(BF16).reshape(nk, CAP, 128)
-
-        @pl.when(y == 0)
-        def _(l=l):
-            ret_self(l).start()
-
-        @pl.when(y != 0)
-        def _(l=l):
-            ret_copy(0, l).start()
-
-        def ret_start(k, c, l=l):
-            ret_copy(k, l).start()
-            return c
-
-        lax.fori_loop(1, nk, ret_start, 0)
-
+        for p in range(2):
+            for j in (1, 3, 2):
+                rs_copy(j, l, p).wait_recv()
+            rs = slice(p * nq // 2, (p + 1) * nq // 2)
+            srcs = [part[y, l, rs]] + [rpart[j - 1, l, rs] for j in (1, 2, 3)]
+            for h in range(feat // 128):
+                cs = slice(h * 128, (h + 1) * 128)
+                val = cols[0][rs] * srcs[0][:, cs].astype(F32)
+                for a in range(1, 4):
+                    val = val + cols[a][rs] * srcs[a][:, cs].astype(F32)
+                ctx[l, p * nk // 2 : (p + 1) * nk // 2, :, cs] = val.astype(BF16).reshape(nk // 2, CAP, 128)
+            part_partners(p, ret_self(l).start, lambda k, l=l: ret_copy(k, l).start())
+
+    share = None
     for l in range(2):
-
-        @pl.when(y == 0)
-        def _(l=l):
-            ret_self(l).wait()
-
-        @pl.when(y != 0)
-        def _(l=l):
-            ret_copy(0, l).wait()
-
-        def ret_wait(k, c, l=l):
-            ret_copy(k, l).wait()
-            return c
-
-        lax.fori_loop(1, nk, ret_wait, 0)
-
-    share = jnp.dot(onehot_t[...], ret[...].reshape(nl * CAP, feat), preferred_element_type=F32) * 0.25
+        all_partners(ret_self(l).wait, lambda k, l=l: ret_copy(k, l).wait_recv())
+        piece = jnp.dot(
+            onehot_t[:, l * nq : (l + 1) * nq], ret[l].reshape(nq, feat), preferred_element_type=F32)
+        share = piece if share is None else share + piece
+
+    share = share * 0.25
     qb = qn // NY
     pq[...] = share.astype(BF16).reshape(NY, qb, feat)
     pq_copies = {}
@@ -419,6 +380,7 @@
     for c in local:
         c.wait()
     mine = q_ref[pl.ds(pl.multiple_of(y * qb, qb), qb), :]
+    hids = [jnp.dot(mine, wi[b, 0:feat, :], preferred_element_type=F32) + bi[b, 0:1, :] for b in range(NY)]
     for j in (1, 2, 3):
         pq_copies[j].wait()
     retrieved = pq[y].astype(F32)
@@ -428,9 +390,8 @@
     normed = normed.astype(BF16)
     res = jnp.zeros((qb, feat), F32)
     for b in range(NY):
-        hid = jnp.dot(mine, wi[b, 0:feat, :], preferred_element_type=F32)
-        hid = hid + jnp.dot(normed, wi[b, feat : 2 * feat, :], preferred_element_type=F32)
-        hid = jax.nn.gelu(hid + bi[b, 0:1, :], approximate=True).astype(BF16)
+        hid = hids[b] + jnp.dot(normed, wi[b, feat : 2 * feat, :], preferred_element_type=F32)
+        hid = jax.nn.gelu(hid, approximate=True).astype(BF16)
         res = res + jnp.dot(hid, wo[b], preferred_element_type=F32)
     ob = feat // NY
     for b in range(NY):
@@ -443,14 +404,27 @@
             device_id=(li, peer(j)), device_id_type=MESH)
         blk_copies[j].start()
     rblk[y] = blk[y]
-    for p in range(2):
+    for l in range(2):
         for j in (1, 3):
-            near_copy(j, p).wait_send()
-        far_copy(p).wait_send()
+            near_copy(j, l).wait_send()
+        for p in range(2):
+            far_copy(p, l).wait_send()
     for j in (1, 2, 3):
         owners_copy(j).wait_send()
     for c in rs_sends:
         c.wait_send()
+    for l in range(2):
+        part_partners(1, None, lambda k, l=l: ret_copy(k, l).wait_send())
+
+        @pl.when(y != 0)
+        def _(l=l):
+            ret_copy(0, l).wait_send()
+
+        def ret_sent(k, c, l=l):
+            ret_copy(k, l).wait_send()
+            return c
+
+        lax.fori_loop(1, nk // 2, ret_sent, 0)
     for j in (1, 2, 3):
         blk_copies[j].wait()
     full = rblk[...].reshape(qn, 128).astype(F32)
@@ -481,11 +455,11 @@
             vm((lists, rows), jnp.int32),
             vm((lists, nt, feat + 16, tile), BF16),
             vm((lists, rows, 128), F32),
-            vm((nk, 2, CAP, qn), BF16),
+            vm((2, nk, CAP, qn), BF16),
             vm((qn, nl * CAP), BF16),
-            vm((nk, 2, CAP, feat), BF16),
+            vm((2, nk, CAP, feat), BF16),
             vm((2, nq), F32),
-            vm((NY, nk, 2, CAP, feat), BF16),
+            vm((NY, 2, nk, CAP, feat), BF16),
             vm((nk, 2, nq), F32),
             vm((NY, 2, nq), F32),
             vm((2, feat, nq), BF16),
@@ -495,8 +469,8 @@
             vm((NY, 2, 1, nq), F32),
             vm((NY - 1, 2, nq, feat), BF16),
             vm((NY - 1, 2, 1, nq), F32),
-            vm((nk, 2, CAP, feat), BF16),
-            vm((nk, 2, CAP, feat), BF16),
+            vm((2, nk, CAP, feat), BF16),
+            vm((2, nk, CAP, feat), BF16),
             vm((NY, qb, feat), BF16),
             vm((NY - 1, qb, feat), BF16),
             vm((NY, qb, 128), BF16),
@@ -505,11 +479,11 @@
             vm((NY, hid, feat), BF16),
             vm((NY, 8, hid), F32),
             dma((3,)),
-            dma((nk,)), dma((nk,)), dma((nk,)), dma((nk,)),
-            dma((3, 2)), dma((3, 2)), dma((3,)), dma((3,)),
+            dma((2, nk)), dma((2, nk)), dma((nk,)), dma((nk,)),
+            dma((3, 2, 2)), dma((3, 2, 2)), dma((3,)), dma((3,)),
             dma((3, 3)), dma((3, 3)),
-            dma((3, 2)), dma((3, 2)), dma((3, 2)), dma((3, 2)),
-            dma((2, 3)), dma((2, 3)), dma((nk, 2)), dma((nk, 2)),
+            dma((3, 2, 2)), dma((3, 2, 2)), dma((3, 2)), dma((3, 2)),
+            dma((2, 3)), dma((2, 3)), dma((2, nk)), dma((2, nk)),
             dma((3,)), dma((3,)), dma((3,)), dma((3,)),
             dma((2,)),
         ],

time: 66.6 us -> 64.6 us (0.970)
  Pallas kernels: 64.2 us -> 62.6 us
    pallas_call x1, Pallas kernels: 64.2 us -> 62.6 us  [body(): pl.pallas_call(kernel, out_shape=jax.ShapeDtypeStruct((feat // NY, qn), B...]
where the time goes in v4:
time: 64.6 us; the launch traced here: 64 us
  Pallas kernels  62.6 us (97%)
  local copies, waits for them, and re-layouts  1.38 us (2%)
    pallas_call x1, Pallas kernels, body(): pl.pallas_call(kernel, out_shape=jax.ShapeDtypeStruct((feat // NY, qn), B...  62.6 us
    unnamed x1, local copies, waits for them, and re-layouts  1.38 us

profile of v4, /device:TPU:32, one launch (start us, length us, event | category | flops | bytes accessed | tf_op | source)
XLA Modules:
  0.0 64.0 jit_solution(17277574564733764948)
XLA Ops:
  0.0 62.6 %shard_map.82 = bf16[64,256]{1,0:T(8,128)(2,1)} custom-call(bf16[256,256]{1,0:T(8,128)(2,1)} %q_ref.1, s32[1,256]{1,0:T(1,128)} %bitcast.5, s32[4,256]{1,0:T(4,128)} %bitcast.4, bf16[2,4096,256]{2,1,0:T(8,128)(2,1)} %slab_hbm.1, s32[2,4096]{1,0:T(2,128)} %rowner_hbm.1, bf16[512,256]{1,0:T(8,128)(2,1)} %win_ref.1, bf16[256]{0:T(256)(128)(2,1)} %bias_ref.1, ...), custom_call_target="tpu_custom_call" | custom-call | tf_op jit(solution)/shard_map/pallas_call | solution.py:448
  62.6 1.4 %copy.10 = bf16[256,64]{0,1:T(8,128)(2,1)} copy(bf16[256,64]{0,1:T(8,128)(2,1)} %bitcast.3) | data formatting | bytes 65536

commit v5 on v4

--- a/solution.py
+++ b/solution.py
@@ -131,7 +131,7 @@
             copy(0)
 
         def step(k, c):
-            copy(k)
+            copy(nk - k)
             return c
 
         lax.fori_loop(1, nk, step, 0)
@@ -298,7 +298,7 @@
             part[psrc, pl_] = mean.T.astype(BF16)
             lse[psrc, pl_] = prev_peak + jnp.log(total)
             if pj != 0:
-                for c in (rl_copy(NY - pj, pl_), rs_copy(NY - pj, pl_, 0), rs_copy(NY - pj, pl_, 1)):
+                for c in (rl_copy(NY - pj, pl_), rs_copy(NY - pj, pl_, 1), rs_copy(NY - pj, pl_, 0)):
                     c.start()
                     rs_sends.append(c)
         if n < len(order):
@@ -326,11 +326,13 @@
             def _():
                 copy(0)
 
+        first, last = max(1, p * nk // 2), (p + 1) * nk // 2
+
         def step(k, c):
-            copy(k)
+            copy(first + last - 1 - k)
             return c
 
-        lax.fori_loop(max(1, p * nk // 2), (p + 1) * nk // 2, step, 0)
+        lax.fori_loop(first, last, step, 0)
 
     for l in range(2):
         for j in (1, 3, 2):
@@ -340,7 +342,7 @@
         es = [jnp.exp(v - top) for v in ls]
         inv = 1.0 / (es[0] + es[1] + es[2] + es[3])
         cols = [jnp.broadcast_to(e * inv, (128, nq)).T for e in es]
-        for p in range(2):
+        for p in (1, 0):
             for j in (1, 3, 2):
                 rs_copy(j, l, p).wait_recv()
             rs = slice(p * nq // 2, (p + 1) * nq // 2)

time: 64.6 us -> 62.6 us (0.969)
  Pallas kernels: 62.6 us -> 60.9 us
    pallas_call x1, Pallas kernels: 62.6 us -> 60.9 us  [body(): pl.pallas_call(kernel, out_shape=jax.ShapeDtypeStruct((feat // NY, qn), B...]
where the time goes in v5:
time: 62.6 us; the launch traced here: 62.3 us
  Pallas kernels  60.9 us (97%)
  local copies, waits for them, and re-layouts  1.38 us (2%)
    pallas_call x1, Pallas kernels, body(): pl.pallas_call(kernel, out_shape=jax.ShapeDtypeStruct((feat // NY, qn), B...  60.9 us
    unnamed x1, local copies, waits for them, and re-layouts  1.38 us

profile of v5, /device:TPU:32, one launch (start us, length us, event | category | flops | bytes accessed | tf_op | source)
XLA Modules:
  0.0 62.3 jit_solution(14596385745465935392)
XLA Ops:
  0.0 60.9 %shard_map.82 = bf16[64,256]{1,0:T(8,128)(2,1)} custom-call(bf16[256,256]{1,0:T(8,128)(2,1)} %q_ref.1, s32[1,256]{1,0:T(1,128)} %bitcast.5, s32[4,256]{1,0:T(4,128)} %bitcast.4, bf16[2,4096,256]{2,1,0:T(8,128)(2,1)} %slab_hbm.1, s32[2,4096]{1,0:T(2,128)} %rowner_hbm.1, bf16[512,256]{1,0:T(8,128)(2,1)} %win_ref.1, bf16[256]{0:T(256)(128)(2,1)} %bias_ref.1, ...), custom_call_target="tpu_custom_call" | custom-call | tf_op jit(solution)/shard_map/pallas_call | solution.py:450
  60.9 1.4 %copy.10 = bf16[256,64]{0,1:T(8,128)(2,1)} copy(bf16[256,64]{0,1:T(8,128)(2,1)} %bitcast.3) | data formatting | bytes 65536

commit v6 on v5

--- a/solution.py
+++ b/solution.py
@@ -304,8 +304,6 @@
         if n < len(order):
             peak = jnp.max(m, axis=0, keepdims=True)
 
-    for j in (1, 3, 2):
-        weight_copies[j][0].start()
 
     def ret_copy(k, l):
         return pltpu.make_async_remote_copy(
@@ -354,6 +352,9 @@
                     val = val + cols[a][rs] * srcs[a][:, cs].astype(F32)
                 ctx[l, p * nk // 2 : (p + 1) * nk // 2, :, cs] = val.astype(BF16).reshape(nk // 2, CAP, 128)
             part_partners(p, ret_self(l).start, lambda k, l=l: ret_copy(k, l).start())
+        if l == 0:
+            for j in (1, 3, 2):
+                weight_copies[j][0].start()
 
     share = None
     for l in range(2):

time: 62.6 us -> 62.5 us (level)
  no operation moved by 1% of the time
where the time goes in v6:
time: 62.5 us; the launch traced here: 62.3 us
  Pallas kernels  60.9 us (97%)
  local copies, waits for them, and re-layouts  1.38 us (2%)
    pallas_call x1, Pallas kernels, body(): pl.pallas_call(kernel, out_shape=jax.ShapeDtypeStruct((feat // NY, qn), B...  60.9 us
    unnamed x1, local copies, waits for them, and re-layouts  1.38 us

profile of v6, /device:TPU:32, one launch (start us, length us, event | category | flops | bytes accessed | tf_op | source)
XLA Modules:
  0.0 62.3 jit_solution(14851843941499877527)
XLA Ops:
  0.0 60.9 %shard_map.82 = bf16[64,256]{1,0:T(8,128)(2,1)} custom-call(bf16[256,256]{1,0:T(8,128)(2,1)} %q_ref.1, s32[1,256]{1,0:T(1,128)} %bitcast.5, s32[4,256]{1,0:T(4,128)} %bitcast.4, bf16[2,4096,256]{2,1,0:T(8,128)(2,1)} %slab_hbm.1, s32[2,4096]{1,0:T(2,128)} %rowner_hbm.1, bf16[512,256]{1,0:T(8,128)(2,1)} %win_ref.1, bf16[256]{0:T(256)(128)(2,1)} %bias_ref.1, ...), custom_call_target="tpu_custom_call" | custom-call | tf_op jit(solution)/shard_map/pallas_call | solution.py:451
  60.9 1.4 %copy.10 = bf16[256,64]{0,1:T(8,128)(2,1)} copy(bf16[256,64]{0,1:T(8,128)(2,1)} %bitcast.3) | data formatting | bytes 65536
